TPU v7x, 512 devices: a whole 4x8x8 slice. The times are simulated.
512 devices in a mesh: fsdp: 16 (over z_lo, x, core), space: 32 (over y, z_hi).
Axes of the slice: x: 4, y: 8, z: 8 (z_hi: 4, z_lo: 2; z = z_hi * 2 + z_lo), core: 2. Of those that a mesh axis runs over, the one named last changes fastest.
Arguments:
- features: bfloat16 [16, 32, 96, 512], P('fsdp', 'space'), may hold values from -6 to 6
- w_first: bfloat16 [96, 2592], P('fsdp'), may hold values from -0.125 to 0.125
- w_second: bfloat16 [96, 2592], P('fsdp'), may hold values from -0.125 to 0.125
- neighbours: int32 [16, 32, 6], P('fsdp', 'space'), may hold values from -1 to 0, as said below
- live_counts: int32 [16, 32], P('fsdp', 'space'), may hold values from 1 to 1, as said below
- output_gradient: bfloat16 [16, 32, 96, 512], P('fsdp', 'space'), may hold values from -6 to 6
Outputs:
- block_out: bfloat16 [16, 32, 96, 512], P('fsdp', 'space')
- grad_in: bfloat16 [16, 32, 96, 512], P('fsdp', 'space')
- grad_first: float32 [96, 2592], P('fsdp')
- grad_second: float32 [96, 2592], P('fsdp')
Inputs may be any that keep to these rules, and one draw needn't show every extreme that they name: `live_counts`: the occupied slots of a device are its first ones; in every scene some device has all 1 slots occupied. Blocks lie on a lattice, device d holding the blocks of one layer along x: the relation is symmetric (if neighbours[s, f] names block r then neighbours[r, f ^ 1] names s), only occupied slots name or are named, and device 0 has none across face 0, device 32 - 1 none across face 1.
All inputs are finite; a program needn't handle non-finite values.
Results may differ from a plain program's by a relative error of at most 0.0054.
Values may be sent and summed in bfloat16 or wider, within the bound.
A program may use at most 64 MiB of HBM per device.

v0:
```python
import jax
import jax.numpy as jnp
from jax import lax
from jax.sharding import PartitionSpec as P

BLOCK_EDGE = 8


epsilon = 1e-05


def extended(block, sides, width):
    for axis, dim in sides:
        count = lax.axis_size(axis)
        forward = [(i, i + 1) for i in range(count - 1)]
        backward = [(target, source) for source, target in forward]
        low = lax.ppermute(
            lax.slice_in_dim(block, block.shape[dim] - width, None, axis=dim), axis, forward
        )
        high = lax.ppermute(lax.slice_in_dim(block, 0, width, axis=dim), axis, backward)
        block = jnp.concatenate([low, block, high], axis=dim)
    return block


def normalize_act(values):
    centre = jnp.mean(values, axis=1, keepdims=True)
    spread = jnp.mean(jnp.square(values - centre), axis=1, keepdims=True)
    return jax.nn.silu((values - centre) * lax.rsqrt(spread + epsilon))


def layer_of(blocks, which_face):
    axis_pos = 2 + which_face // 2
    index_pos = 0 if which_face % 2 == 0 else blocks.shape[axis_pos] - 1
    return lax.index_in_dim(blocks, index_pos, axis_pos, keepdims=False)


def with_margins(blocks, pulled):
    edge_len = blocks.shape[2]
    padded = jnp.pad(blocks, ((0, 0), (0, 0), (1, 1), (1, 1), (1, 1)))
    middle = slice(1, edge_len + 1)
    padded = padded.at[:, :, 0, middle, middle].set(pulled[0])
    padded = padded.at[:, :, edge_len + 1, middle, middle].set(pulled[1])
    padded = padded.at[:, :, middle, 0, middle].set(pulled[2])
    padded = padded.at[:, :, middle, edge_len + 1, middle].set(pulled[3])
    padded = padded.at[:, :, middle, middle, 0].set(pulled[4])
    padded = padded.at[:, :, middle, middle, edge_len + 1].set(pulled[5])
    return padded


def unfold(padded, edge_len):
    columns = []
    for shift_x in range(3):
        for shift_y in range(3):
            for shift_z in range(3):
                columns.append(
                    padded[
                        :,
                        :,
                        shift_x : shift_x + edge_len,
                        shift_y : shift_y + edge_len,
                        shift_z : shift_z + edge_len,
                    ]
                )
    stacked = jnp.stack(columns, axis=1)
    return stacked.reshape(padded.shape[0], 27 * padded.shape[1], edge_len**3)


def flipped(weight):
    channels = weight.shape[0]
    tap_major = weight.reshape(channels, 27, channels)[:, ::-1, :]
    return jnp.transpose(tap_major, (2, 1, 0)).reshape(channels, 27 * channels)


def neighbour_faces(blocks, near_slots):
    slot_total = blocks.shape[0]
    layers_flat = [layer_of(blocks, which_face).reshape(slot_total, -1) for which_face in range(6)]
    outward = jnp.stack([layers_flat[0], layers_flat[1]])[None]
    beside = extended(outward, (("space", 0),), 1)
    sources = [
        beside[0, 1],
        beside[2, 0],
        layers_flat[3],
        layers_flat[2],
        layers_flat[5],
        layers_flat[4],
    ]
    slot_ids = jnp.arange(slot_total)
    pulled = []
    for which_face in range(6):
        picker = (near_slots[:, which_face][:, None] == slot_ids[None, :]).astype(blocks.dtype)
        fetched = jnp.dot(picker, sources[which_face], preferred_element_type=jnp.float32).astype(
            blocks.dtype
        )
        pulled.append(fetched.reshape(slot_total, blocks.shape[1], BLOCK_EDGE, BLOCK_EDGE))
    return pulled


def convolve(weight, flat_blocks, near_slots):
    slot_total, channels = (flat_blocks.shape[0], flat_blocks.shape[1])
    cube_blocks = flat_blocks.reshape(slot_total, channels, BLOCK_EDGE, BLOCK_EDGE, BLOCK_EDGE)
    columns = unfold(
        with_margins(cube_blocks, neighbour_faces(cube_blocks, near_slots)), BLOCK_EDGE
    )
    result = jnp.einsum("ok,bkv->bov", weight, columns, preferred_element_type=jnp.float32)
    return (result, columns)


def body(features, w_first, w_second, neighbours, live_counts, output_gradient):
    blocks_in = features[0]
    near_slots = neighbours[0]
    grad_top = output_gradient[0]
    slot_total = blocks_in.shape[0]
    occupied = (jnp.arange(slot_total) < live_counts[0, 0]).astype(jnp.float32)[:, None, None]
    weight_one, weight_two = (
        lax.all_gather(w_first, "fsdp", axis=0, tiled=True),
        lax.all_gather(w_second, "fsdp", axis=0, tiled=True),
    )
    inputs_f32 = blocks_in.astype(jnp.float32)
    act_first, pull_first = jax.vjp(normalize_act, inputs_f32)
    active_one = (act_first * occupied).astype(jnp.bfloat16)
    hidden, cols_one = convolve(weight_one, active_one, near_slots)
    act_second, pull_second = jax.vjp(normalize_act, hidden)
    active_two = (act_second * occupied).astype(jnp.bfloat16)
    branch_out, cols_two = convolve(weight_two, active_two, near_slots)
    block_out = ((inputs_f32 + branch_out) * occupied).astype(jnp.bfloat16)
    grad_two = (grad_top.astype(jnp.float32) * occupied).astype(jnp.bfloat16)
    term_two = jnp.einsum("bov,bkv->ok", grad_two, cols_two, preferred_element_type=jnp.float32)
    weight_one, weight_two = (
        lax.all_gather(w_first, "fsdp", axis=0, tiled=True),
        lax.all_gather(w_second, "fsdp", axis=0, tiled=True),
    )
    back_two = convolve(flipped(weight_two), grad_two, near_slots)[0]
    grad_hidden = pull_second(back_two * occupied)[0]
    grad_one = (grad_hidden * occupied).astype(jnp.bfloat16)
    term_one = jnp.einsum("bov,bkv->ok", grad_one, cols_one, preferred_element_type=jnp.float32)
    back_one = convolve(flipped(weight_one), grad_one, near_slots)[0]
    grad_input = pull_first(back_one * occupied)[0]
    grad_in = ((grad_top.astype(jnp.float32) + grad_input) * occupied).astype(jnp.bfloat16)
    total_one, total_two = lax.psum((term_one, term_two), "space")
    share_one, share_two = (
        lax.psum_scatter(total_one, "fsdp", scatter_dimension=0, tiled=True),
        lax.psum_scatter(total_two, "fsdp", scatter_dimension=0, tiled=True),
    )
    return (block_out[None], grad_in[None], share_one, share_two)


def solution(mesh):
    placed = (
        P("fsdp", "space", None, None),
        P("fsdp", None),
        P("fsdp", None),
        P("fsdp", "space", None),
        P("fsdp", "space"),
        P("fsdp", "space", None, None),
    )
    return jax.shard_map(
        body,
        mesh=mesh,
        in_specs=placed,
        out_specs=(
            P("fsdp", "space", None, None),
            P("fsdp", "space", None, None),
            P("fsdp", None),
            P("fsdp", None),
        ),
        check_vma=False,
    )
```

profile of v0, /device:TPU:4, one launch (start us, length us, event | category | flops | bytes accessed | tf_op | source)
XLA Modules:
  0.0 642.4 jit_solution(303272749665601640)
XLA Ops:
  7.9 0.9 fusion.10
  10.4 6.7 %collective-permute-start.4 = (bf16[1,2,1,6144]{3,1,2,0:T(2,128)(2,1)}, bf16[1,2,1,6144]{3,1,2,0:T(2,128)(2,1)}, u32[]{:S(2)}, u32[]{:S(2)}) collective-permute-start(bf16[1,2,1,6144]{3,1,2,0:T(2,128)(2,1)} %maximum_bitcast_fusion.1), channel_id=1, source_target_pairs={{0,1},{1,2},{2,3},{3,4},{4,5},{5,6},{6,7},{7,8},{8,9},{9,10},{10,1... | collective-permute-start | bytes 73736 | tf_op jit(solution)/shard_map/ppermute | solution.py:17
  17.1 1.3 collective-permute-start.5
  18.3 0.9 convert_reduce_fusion
  19.3 0.9 multiply_reduce_fusion.1
  20.3 1.0 copy.137
  23.3 7.9 %collective-permute-start = (bf16[1,2,1,6144]{3,1,2,0:T(2,128)(2,1)}, bf16[1,2,1,6144]{3,1,2,0:T(2,128)(2,1)}, u32[]{:S(2)}, u32[]{:S(2)}) collective-permute-start(bf16[1,2,1,6144]{3,1,2,0:T(2,128)(2,1)} %bitcast.605), channel_id=1, source_target_pairs={{0,1},{1,2},{2,3},{3,4},{4,5},{5,6},{6,7},{7,8},{8,9},{9,10},{10,1... | collective-permute-start | bytes 73736 | tf_op jit(solution)/shard_map/ppermute | solution.py:17
  31.2 1.3 collective-permute-start.1
  37.6 18.4 %all-gather = bf16[16,6,2592]{2,1,0:T(8,128)(2,1)S(1)} all-gather(bf16[1,6,2592]{2,1,0:T(8,128)(2,1)S(1)} %bitcast.629), channel_id=1, replica_groups=mesh['fsdp'=16,'space'=32] {'fsdp'}, dimensions={0}, use_global_device_ids=true | all-gather | bytes 528768 | tf_op jit(solution)/shard_map/all_gather | solution.py:115
  56.0 18.1 %all-gather.1 = bf16[16,6,2592]{2,1,0:T(8,128)(2,1)S(1)} all-gather(bf16[1,6,2592]{2,1,0:T(8,128)(2,1)S(1)} %bitcast.630), channel_id=1, replica_groups=mesh['fsdp'=16,'space'=32] {'fsdp'}, dimensions={0}, use_global_device_ids=true | all-gather | bytes 528768 | tf_op jit(solution)/shard_map/all_gather | solution.py:116
  75.3 0.9 reshape.1928
  76.2 1.8 reshape.1922
  78.0 1.1 reshape.1943
  80.4 0.7 copy.176
  81.2 2.3 rev.6
  83.5 1.1 copy.178
  84.6 0.8 rev.7
  85.4 1.1 copy.195
  86.5 1.3 dynamic-slice.174
  88.4 0.8 fusion.47
  89.6 0.8 fusion.48
  93.6 0.8 fusion.43
  94.5 5.9 copy.177
  100.4 8.1 %reshape.1921 = bf16[2592,512]{0,1:T(8,128)(2,1)} reshape(bf16[1,27,96,8,8,8]{2,1,5,4,3,0:T(8,128)(2,1)} %copy.177) | data formatting | bytes 5308416 | tf_op jit(solution)/shard_map/reshape.1073
  108.9 0.8 fusion.44
  113.2 4.4 copy.145
  117.6 6.9 %reshape.1914 = bf16[2592,512]{0,1:T(8,128)(2,1)S(1)} reshape(bf16[1,27,96,8,8,8]{2,1,5,4,3,0:T(8,128)(2,1)} %copy.145) | data formatting | bytes 5308416 | tf_op jit(solution)/shard_map/reshape.994
  124.6 1.0 fusion.61
  125.6 0.7 copy-done.1
  126.5 1.0 multiply_reduce_fusion.4
  127.7 1.6 fusion.21
  130.5 6.1 collective-permute-start.2
  136.6 1.3 collective-permute-start.3
  139.4 6.6 %collective-permute-start.6 = (bf16[1,2,1,6144]{3,1,2,0:T(2,128)(2,1)}, bf16[1,2,1,6144]{3,1,2,0:T(2,128)(2,1)S(1)}, u32[]{:S(2)}, u32[]{:S(2)}) collective-permute-start(bf16[1,2,1,6144]{3,1,2,0:T(2,128)(2,1)} %maximum_bitcast_fusion.2), channel_id=1, source_target_pairs={{0,1},{1,2},{2,3},{3,4},{4,5},{5,6},{6,7},{7,8},{8,9},{9,10},{10,1... | collective-permute-start | bytes 73736 | tf_op jit(solution)/shard_map/ppermute | solution.py:17
  146.1 1.3 collective-permute-start.7
  151.3 5.9 copy.161
  157.2 7.0 %reshape.1918 = bf16[2592,512]{0,1:T(8,128)(2,1)S(1)} reshape(bf16[1,27,96,8,8,8]{2,1,5,4,3,0:T(8,128)(2,1)} %copy.161) | data formatting | bytes 5308416 | tf_op jit(solution)/shard_map/reshape.1034
  164.2 1.6 fusion.19
  186.6 7.9 %copy.194 = bf16[1,27,96,8,8,8]{2,1,5,4,3,0:T(8,128)(2,1)} copy(bf16[1,27,96,8,8,8]{2,5,4,3,1,0:T(8,128)(2,1)} %constant_dynamic-update-slice_fusion.81) | data formatting | bytes 5308416 | tf_op jit(solution)/shard_map/stack | solution.py:64
  194.6 8.1 %reshape.1927 = bf16[2592,512]{0,1:T(8,128)(2,1)} reshape(bf16[1,27,96,8,8,8]{2,1,5,4,3,0:T(8,128)(2,1)} %copy.194) | data formatting | bytes 5308416 | tf_op jit(solution)/shard_map/reshape.1119
  202.7 3.0 multiply_reduce_fusion.3
  205.8 1.6 fusion.5
  207.4 112.7 %all-reduce.13.cloned.1.call-done = (f32[96,2592]{1,0:T(8,128)}, f32[96,2592]{1,0:T(8,128)}) async-done(((f32[96,2592]{1,0:T(8,128)}, f32[96,2592]{1,0:T(8,128)}), (f32[96,2592]{1,0:T(8,128)}, f32[96,2592]{1,0:T(8,128)})) %all-reduce.13.cloned.1.call-update) | async-done | bytes 1990672
  320.1 1.6 constant_dynamic-slice_fusion
  321.7 1.6 constant_dynamic-slice_fusion.1
  324.0 308.2 %all-reduce.11.cloned.1.call-done = (f32[6,2592]{1,0:T(8,128)}, f32[6,2592]{1,0:T(8,128)}) async-done(((f32[6,2592]{1,0:T(8,128)}, f32[6,2592]{1,0:T(8,128)}), (f32[6,2592]{1,0:T(8,128)}, f32[6,2592]{1,0:T(8,128)})) %all-reduce.11.cloned.1.call-update) | async-done | bytes 124432 | tf_op jit(solution)/shard_map/psum | solution.py:139
  632.2 1.5 copy.361
  633.8 1.5 copy.362
  (265 shorter events, 42.6 us)
Async XLA Ops:
  7.2 25.4 %copy-start.16 = (s32[1,1,6]{2,1,0:T(1,128)S(1)}, s32[1,1,6]{2,1,0:T(1,128)}, u32[]{:S(2)}) copy-start(s32[1,1,6]{2,1,0:T(1,128)} %param.57) | copy-start | bytes 76
  7.2 30.5 %copy-start.12 = (bf16[6,2592]{1,0:T(8,128)(2,1)S(1)}, bf16[6,2592]{1,0:T(8,128)(2,1)}, u32[]{:S(2)}) copy-start(bf16[6,2592]{1,0:T(8,128)(2,1)} %param.55) | copy-start | bytes 93316
  7.2 48.8 %copy-start.13 = (bf16[6,2592]{1,0:T(8,128)(2,1)S(1)}, bf16[6,2592]{1,0:T(8,128)(2,1)}, u32[]{:S(2)}) copy-start(bf16[6,2592]{1,0:T(8,128)(2,1)} %param.56) | copy-start | bytes 93316
  7.2 312.9 %all-reduce.13.cloned.1.call-start = ((), (), s32[]{:S(2)}) async-start(), calls=%async_computation.1 | async-start | bytes 4128768
  8.8 11.4 %copy-start.3 = (bf16[1,1,96,512]{3,2,1,0:T(8,128)(2,1)}, bf16[1,1,96,512]{3,2,1,0:T(8,128)(2,1)S(1)}, u32[]{:S(2)}) copy-start(bf16[1,1,96,512]{3,2,1,0:T(8,128)(2,1)S(1)} %fusion.10) | copy-start | bytes 294916
  10.4 78.0 %collective-permute-start.4 = (bf16[1,2,1,6144]{3,1,2,0:T(2,128)(2,1)}, bf16[1,2,1,6144]{3,1,2,0:T(2,128)(2,1)}, u32[]{:S(2)}, u32[]{:S(2)}) collective-permute-start(bf16[1,2,1,6144]{3,1,2,0:T(2,128)(2,1)} %maximum_bitcast_fusion.1), channel_id=1, source_target_pairs={{0,1},{1,2},{2,3},{3,4},{4,5},{5,6},{6,7},{7,8},{8,9},{9,10},{10,1... | collective-permute-start | bytes 73736 | tf_op jit(solution)/shard_map/ppermute | solution.py:17
  17.1 72.6 %collective-permute-start.5 = (bf16[1,2,1,6144]{3,1,2,0:T(2,128)(2,1)}, bf16[1,2,1,6144]{3,1,2,0:T(2,128)(2,1)}, u32[]{:S(2)}, u32[]{:S(2)}) collective-permute-start(bf16[1,2,1,6144]{3,1,2,0:T(2,128)(2,1)} %maximum_bitcast_fusion.1), channel_id=1, source_target_pairs={{1,0},{2,1},{3,2},{4,3},{5,4},{6,5},{7,6},{8,7},{9,8},{10,9},{11,1... | collective-permute-start | bytes 73736 | tf_op jit(solution)/shard_map/ppermute | solution.py:20
  20.2 1.1 copy-start.14
  23.3 70.3 %collective-permute-start = (bf16[1,2,1,6144]{3,1,2,0:T(2,128)(2,1)}, bf16[1,2,1,6144]{3,1,2,0:T(2,128)(2,1)}, u32[]{:S(2)}, u32[]{:S(2)}) collective-permute-start(bf16[1,2,1,6144]{3,1,2,0:T(2,128)(2,1)} %bitcast.605), channel_id=1, source_target_pairs={{0,1},{1,2},{2,3},{3,4},{4,5},{5,6},{6,7},{7,8},{8,9},{9,10},{10,1... | collective-permute-start | bytes 73736 | tf_op jit(solution)/shard_map/ppermute | solution.py:17
  31.2 77.7 %collective-permute-start.1 = (bf16[1,2,1,6144]{3,1,2,0:T(2,128)(2,1)}, bf16[1,2,1,6144]{3,1,2,0:T(2,128)(2,1)}, u32[]{:S(2)}, u32[]{:S(2)}) collective-permute-start(bf16[1,2,1,6144]{3,1,2,0:T(2,128)(2,1)} %bitcast.605), channel_id=1, source_target_pairs={{1,0},{2,1},{3,2},{4,3},{5,4},{6,5},{7,6},{8,7},{9,8},{10,9},{11,1... | collective-permute-start | bytes 73736 | tf_op jit(solution)/shard_map/ppermute | solution.py:20
  81.2 9.9 %copy-start.11 = (bf16[1,96,8,1,8]{1,4,3,2,0:T(8,128)(2,1)S(1)}, bf16[1,96,8,1,8]{1,4,3,2,0:T(8,128)(2,1)}, u32[]{:S(2)}) copy-start(bf16[1,96,8,1,8]{1,4,3,2,0:T(8,128)(2,1)} %get-tuple-element.311) | copy-start | bytes 36868
  81.2 10.1 %copy-start.10 = (bf16[1,96,8,1,8]{1,4,3,2,0:T(8,128)(2,1)S(1)}, bf16[1,96,8,1,8]{1,4,3,2,0:T(8,128)(2,1)}, u32[]{:S(2)}) copy-start(bf16[1,96,8,1,8]{1,4,3,2,0:T(8,128)(2,1)} %get-tuple-element.310) | copy-start | bytes 36868
  100.4 10.0 %copy-start.7 = (bf16[1,96,8,1,8]{1,3,4,2,0:T(2,128)(2,1)S(1)}, bf16[1,96,8,1,8]{1,3,4,2,0:T(2,128)(2,1)}, u32[]{:S(2)}) copy-start(bf16[1,96,8,1,8]{1,3,4,2,0:T(2,128)(2,1)} %get-tuple-element.323) | copy-start | bytes 36868
  100.4 10.9 %copy-start.9 = (bf16[1,96,8,8,1]{1,3,4,2,0:T(8,128)(2,1)S(1)}, bf16[1,96,8,8,1]{1,3,4,2,0:T(8,128)(2,1)}, u32[]{:S(2)}) copy-start(bf16[1,96,8,8,1]{1,3,4,2,0:T(8,128)(2,1)} %get-tuple-element.321) | copy-start | bytes 36868
  100.4 11.1 %copy-start.8 = (bf16[1,96,8,8,1]{1,3,4,2,0:T(8,128)(2,1)S(1)}, bf16[1,96,8,8,1]{1,3,4,2,0:T(8,128)(2,1)}, u32[]{:S(2)}) copy-start(bf16[1,96,8,8,1]{1,3,4,2,0:T(8,128)(2,1)} %get-tuple-element.320) | copy-start | bytes 36868
  124.5 1.8 copy-start.1
  124.5 1.9 copy-start.5
  130.5 17.1 %collective-permute-start.2 = (bf16[1,2,1,6144]{3,1,2,0:T(2,128)(2,1)S(1)}, bf16[1,2,1,6144]{3,1,2,0:T(2,128)(2,1)S(1)}, u32[]{:S(2)}, u32[]{:S(2)}) collective-permute-start(bf16[1,2,1,6144]{3,1,2,0:T(2,128)(2,1)S(1)} %maximum_bitcast_fusion), channel_id=1, source_target_pairs={{0,1},{1,2},{2,3},{3,4},{4,5},{5,6},{6,7},{7,8},{8,9},{9,10},{10,1... | collective-permute-start | bytes 73736 | tf_op jit(solution)/shard_map/ppermute | solution.py:17
  136.6 11.6 %collective-permute-start.3 = (bf16[1,2,1,6144]{3,1,2,0:T(2,128)(2,1)S(1)}, bf16[1,2,1,6144]{3,1,2,0:T(2,128)(2,1)S(1)}, u32[]{:S(2)}, u32[]{:S(2)}) collective-permute-start(bf16[1,2,1,6144]{3,1,2,0:T(2,128)(2,1)S(1)} %maximum_bitcast_fusion), channel_id=1, source_target_pairs={{1,0},{2,1},{3,2},{4,3},{5,4},{6,5},{7,6},{8,7},{9,8},{10,9},{11,1... | collective-permute-start | bytes 73736 | tf_op jit(solution)/shard_map/ppermute | solution.py:20
  139.4 26.4 %collective-permute-start.6 = (bf16[1,2,1,6144]{3,1,2,0:T(2,128)(2,1)}, bf16[1,2,1,6144]{3,1,2,0:T(2,128)(2,1)S(1)}, u32[]{:S(2)}, u32[]{:S(2)}) collective-permute-start(bf16[1,2,1,6144]{3,1,2,0:T(2,128)(2,1)} %maximum_bitcast_fusion.2), channel_id=1, source_target_pairs={{0,1},{1,2},{2,3},{3,4},{4,5},{5,6},{6,7},{7,8},{8,9},{9,10},{10,1... | collective-permute-start | bytes 73736 | tf_op jit(solution)/shard_map/ppermute | solution.py:17
  146.1 20.3 %collective-permute-start.7 = (bf16[1,2,1,6144]{3,1,2,0:T(2,128)(2,1)}, bf16[1,2,1,6144]{3,1,2,0:T(2,128)(2,1)S(1)}, u32[]{:S(2)}, u32[]{:S(2)}) collective-permute-start(bf16[1,2,1,6144]{3,1,2,0:T(2,128)(2,1)} %maximum_bitcast_fusion.2), channel_id=1, source_target_pairs={{1,0},{2,1},{3,2},{4,3},{5,4},{6,5},{7,6},{8,7},{9,8},{10,9},{11,1... | collective-permute-start | bytes 73736 | tf_op jit(solution)/shard_map/ppermute | solution.py:20
  157.2 7.0 %copy-start.4 = (bf16[1,1,96,512]{3,2,1,0:T(8,128)(2,1)S(1)}, bf16[1,1,96,512]{3,2,1,0:T(8,128)(2,1)}, u32[]{:S(2)}) copy-start(bf16[1,1,96,512]{3,2,1,0:T(8,128)(2,1)} %copy-done.3) | copy-start | bytes 294916
  183.6 448.6 %all-reduce.11.cloned.1.call-start = ((), (), s32[]{:S(2)}) async-start(), calls=%async_computation | async-start | bytes 344064 | tf_op jit(solution)/shard_map/psum | solution.py:139
  194.6 8.1 %copy-start = (bf16[1,1,96,512]{3,2,1,0:T(8,128)(2,1)S(1)}, bf16[1,1,96,512]{3,2,1,0:T(8,128)(2,1)}, u32[]{:S(2)}) copy-start(bf16[1,1,96,512]{3,2,1,0:T(8,128)(2,1)} %param.54) | copy-start | bytes 294916
  202.7 3.0 copy-start.15
  202.7 3.1 copy-start.2
  205.7 117.6 %copy-start.6 = (bf16[1,1,96,512]{3,2,1,0:T(8,128)(2,1)S(1)}, bf16[1,1,96,512]{3,2,1,0:T(8,128)(2,1)}, u32[]{:S(2)}) copy-start(bf16[1,1,96,512]{3,2,1,0:T(8,128)(2,1)} %param.59) | copy-start | bytes 294916
Sparse Core Ops, SparseCore 0:
  183.7 136.3 all-reduce.12
  323.7 308.4 all-reduce.10
where the time goes:
time: 650 us; the launch traced here: 642 us
  waiting for transfers between devices  421 us (65%)
  local copies, waits for them, and re-layouts  110 us (17%)
  blocking collectives  36.5 us (6%)
  starting transfers between devices  32.8 us (5%)
  between operations  20.4 us (3%)
  other arithmetic  11.7 us (2%)
  matrix products  9.86 us (2%)
    psum x1, waiting for transfers between devices, body(): total_one, total_two = lax.psum((term_one, term_two), 'space')  308 us
    unnamed x3, waiting for transfers between devices  113 us
    another operation x20, local copies, waits for them, and re-layouts  33.4 us
    unnamed x146, local copies, waits for them, and re-layouts  32.5 us
    ppermute x4, starting transfers between devices, extended(): lax.ppermute(lax.slice_in_dim(block, block.shape[dim] - width, None, axis...  27.3 us
    another operation x8, local copies, waits for them, and re-layouts, unfold(): stacked = jnp.stack(columns, axis=1)  25.1 us
    all_gather x1, blocking collectives, body(): lax.all_gather(w_first, 'fsdp', axis=0, tiled=True)  18.4 us
    all_gather x1, blocking collectives, body(): lax.all_gather(w_second, 'fsdp', axis=0, tiled=True)  18.1 us
  transfers between devices with their start and end apart: 10, of which 2 were waited for; matrix products, arithmetic and copies ran while one was open for 13% of the time, Pallas kernels for 0%

commit v1 on v0

v1 whole, which is shorter than its diff:
```python
import jax
import jax.numpy as jnp
from jax import lax
from jax.experimental import pallas as pl
from jax.experimental.pallas import tpu as pltpu
from jax.sharding import PartitionSpec as P

MESH = pl.DeviceIdType.MESH
F32 = jnp.float32
BF16 = jnp.bfloat16

CH = 96
LT = 128
KA = 9 * CH
KP = 896
HALF = 11 * LT
EPS = 1e-05


def xor(value, pattern):
    for bit in (1, 2, 4):
        if pattern & bit:
            value = value + (1 - 2 * lax.rem(lax.div(value, bit), 2)) * bit
    return value


def half_turn(tile):
    return pltpu.roll(tile, 64, 1)


def paired(tiles, low):
    t0, t1, t2, t3 = tiles
    return (
        jnp.where(low, t0, half_turn(t2)),
        jnp.where(low, half_turn(t0), t2),
        jnp.where(low, t1, half_turn(t3)),
        jnp.where(low, half_turn(t1), t3),
    )


def unpaired(tiles, low):
    p0, p1, p2, p3 = tiles
    return (
        jnp.where(low, p0, half_turn(p1)),
        jnp.where(low, p2, half_turn(p3)),
        jnp.where(low, half_turn(p0), p1),
        jnp.where(low, half_turn(p2), p3),
    )


def normalized(u):
    centred = u - jnp.mean(u, axis=0, keepdims=True)
    scale = lax.rsqrt(jnp.mean(centred * centred, axis=0, keepdims=True) + EPS)
    return centred * scale, scale


def sigmoid(v):
    return 1.0 / (1.0 + jnp.exp(-v))


def act_vjp(norm, scale, cotangent):
    gate = sigmoid(norm)
    inner = cotangent * (gate * (1.0 + norm * (1.0 - gate)))
    return scale * (
        inner
        - jnp.mean(inner, axis=0, keepdims=True)
        - norm * jnp.mean(inner * norm, axis=0, keepdims=True)
    )


def kernel(
    feat_ref, wone_ref, wtwo_ref, near_ref, live_ref, grad_ref,
    bout_ref, gin_ref, gone_ref, gtwo_ref,
    w_buf, w_full, w_flip, halo_out, halo_in, cols, x_buf, n_buf, r_buf, gp_buf,
    term, one_out, one_in, two_out, two_in, sum_src, sum_in, piece, piece_in, whole,
    w_send, w_recv, f_send, f_recv, halo_send, halo_recv,
    one_send, one_recv, two_send, two_recv, y_send, y_recv, z_send, z_recv, g_send, g_recv,
):
    fsdp = lax.axis_index("fsdp")
    space = lax.axis_index("space")
    chip, core = lax.div(fsdp, 2), lax.rem(fsdp, 2)
    row, col = lax.div(space, 4), lax.rem(space, 4)
    sibling = {"fsdp": chip * 2 + (1 - core), "space": space}

    def chip_mate(j):
        return {"fsdp": xor(chip, j) * 2 + core, "space": space}

    def row_mate(j):
        return {"fsdp": fsdp, "space": xor(row, j) * 4 + col}

    def col_mate(j):
        return {"fsdp": fsdp, "space": row * 4 + xor(col, j)}

    below = {"fsdp": fsdp, "space": lax.rem(space + 31, 32)}
    above = {"fsdp": fsdp, "space": lax.rem(space + 1, 32)}

    mates = (
        [sibling, below, above]
        + [chip_mate(j) for j in range(1, 8)]
        + [row_mate(j) for j in range(1, 8)]
        + [col_mate(j) for j in range(1, 4)]
    )
    barrier = pltpu.get_barrier_semaphore()
    for mate in mates:
        pl.semaphore_signal(barrier, inc=1, device_id=mate, device_id_type=MESH)

    sent = []

    def send(src, dst, send_sem, recv_sem, device):
        copy = pltpu.make_async_remote_copy(
            src_ref=src, dst_ref=dst, send_sem=send_sem, recv_sem=recv_sem,
            device_id=device, device_id_type=MESH,
        )
        copy.start()
        sent.append(copy)
        return copy

    for k, ref in enumerate((wone_ref, wtwo_ref)):
        rows = ref[...].astype(F32)
        gap = jnp.zeros((6, KP - KA), F32)
        parts = []
        for a in range(3):
            parts += [rows[:, a * KA : (a + 1) * KA], gap]
        flat = jnp.concatenate(parts + [jnp.zeros((6, LT), F32)], axis=1)
        flat = jnp.concatenate([flat, jnp.zeros((2, 2 * HALF), F32)], axis=0)
        w_buf[k, 0] = jnp.concatenate([flat[:, :HALF], flat[:, HALF:]], axis=0).astype(BF16)

    pl.semaphore_wait(barrier, len(mates))

    w_copy, f_copy = [], []
    for k in range(2):
        own = [send(w_buf.at[k, 0], w_buf.at[k, 8], f_send.at[k, 0], f_recv.at[k, 0], sibling)]
        f_copy.append(own)
        w_copy.append([
            send(w_buf.at[k, 0], w_buf.at[k, j], w_send.at[k, j - 1], w_recv.at[k, j - 1], chip_mate(j))
            for j in range(1, 8)
        ])

    def forward_weight(k):
        for j in range(1, 8):
            w_copy[k][j - 1].wait_recv()
            f_copy[k].append(
                send(w_buf.at[k, j], w_buf.at[k, 8 + j], f_send.at[k, j], f_recv.at[k, j], sibling)
            )

    lane = lax.broadcasted_iota(jnp.int32, (1, LT), 1)
    z_pos, y_pos = lane & 7, (lane >> 3) & 7
    low = lane < 64

    def flag(cond):
        return jnp.where(cond, 1.0, 0.0).astype(F32)

    def named(face):
        return jnp.where(near_ref[0, 0, face] >= 0, 1.0, 0.0).astype(F32)

    occupied = jnp.where(live_ref[0, 0] > 0, 1.0, 0.0).astype(F32)
    low_f, high_f = flag(low), flag(lane >= 64)
    in_z = {c: flag((z_pos + c - 1 >= 0) & (z_pos + c - 1 < 8)) for c in (0, 2)}
    in_y = {b: flag((y_pos + b - 1 >= 0) & (y_pos + b - 1 < 8)) for b in (0, 2)}

    def wide(mask):
        return jnp.broadcast_to(mask, (CH, LT)).astype(BF16)

    inside = {"low": high_f, "mid": jnp.ones((1, LT), F32), "high": low_f}
    z_keep = {c: wide(in_z[c]) for c in (0, 2)}
    y_keep = {b: wide(in_y[b]) for b in (0, 2)}
    z_wrap = {
        (c, w): wide((1.0 - in_z[c]) * named(4 + c // 2) * inside[w]) for c in (0, 2) for w in inside
    }
    y_wrap = {}
    for b in (0, 2):
        for w in inside:
            base = (1.0 - in_y[b]) * named(2 + b // 2) * inside[w]
            for c in range(3):
                y_wrap[b, c, w] = wide(base if c == 1 else base * in_z[c])

    def unroll_tile(which, j, tile):
        w = "low" if j == 0 else "high" if j == 5 else "mid"
        for c in range(3):
            if c == 1:
                along = tile
            else:
                dz = c - 1
                along = (
                    pltpu.roll(tile, -dz % LT, 1) * z_keep[c]
                    + pltpu.roll(tile, 7 * dz % LT, 1) * z_wrap[c, w]
                )
            for b in range(3):
                if b == 1:
                    both = along
                else:
                    dy = b - 1
                    both = (
                        pltpu.roll(along, -8 * dy % LT, 1) * y_keep[b]
                        + pltpu.roll(along, 56 * dy % LT, 1) * y_wrap[b, c, w]
                    )
                tap = b * 3 + c
                cols[which, tap * CH : (tap + 1) * CH, j * LT : (j + 1) * LT] = both

    halo_copy = {}

    def send_halo(which, first, last):
        halo_out[which, 0] = half_turn(first)
        halo_out[which, 1] = half_turn(last)
        halo_copy[which] = [
            send(halo_out.at[which, 0], halo_in.at[which, 0], halo_send.at[which, 0],
                 halo_recv.at[which, 0], below),
            send(halo_out.at[which, 1], halo_in.at[which, 1], halo_send.at[which, 1],
                 halo_recv.at[which, 1], above),
        ]

    def unroll_middle(which, tiles):
        cols[which, KA:KP, :] = jnp.zeros((KP - KA, 6 * LT), BF16)
        for j in range(4):
            unroll_tile(which, j + 1, tiles[j])

    def unroll_edges(which):
        for copy in halo_copy[which]:
            copy.wait_recv()
        lower = halo_out[which, 1] * wide(high_f) + halo_in[which, 1] * wide(low_f * named(0))
        unroll_tile(which, 0, lower)
        upper = halo_out[which, 0] * wide(low_f) + halo_in[which, 0] * wide(high_f * named(1))
        unroll_tile(which, 5, upper)

    def lanes_of(array, j):
        return array[:, j * LT : (j + 1) * LT]

    x_tiles = paired([feat_ref[0, 0, :, j * LT : (j + 1) * LT].astype(F32) for j in range(4)], low)
    a_one = []
    for j in range(4):
        norm, scale = normalized(x_tiles[j])
        x_buf[0, j] = x_tiles[j]
        n_buf[0, j], r_buf[0, j] = norm, scale
        a_one.append((occupied * (norm * sigmoid(norm))).astype(BF16))
    send_halo(0, a_one[0], a_one[3])
    g_tiles = paired([grad_ref[0, 0, :, j * LT : (j + 1) * LT].astype(F32) for j in range(4)], low)
    g_two = []
    for j in range(4):
        x_buf[1, j] = g_tiles[j]
        g_two.append((occupied * g_tiles[j]).astype(BF16))
    send_halo(1, g_two[0], g_two[3])
    unroll_middle(0, a_one)
    unroll_middle(1, g_two)

    r_row = lax.broadcasted_iota(jnp.int32, (LT, CH), 0)
    r_col = lax.broadcasted_iota(jnp.int32, (LT, CH), 1)
    r_core = core + (r_row >> 6) * (1 - 2 * core)
    r_owner = (((r_row >> 3) & 7) ^ chip) * 2 + r_core
    spread = jnp.where(((r_row & 7) < 6) & (r_owner * 6 + (r_row & 7) == r_col), 1.0, 0.0).astype(BF16)

    def spread_rows(tiles):
        whole_g = jnp.concatenate(list(tiles), axis=1)
        return jnp.dot(spread, whole_g, preferred_element_type=F32).astype(BF16)

    gp_buf[1] = spread_rows(g_two)

    p_row = lax.broadcasted_iota(jnp.int32, (2 * CH, 256), 0)
    p_col = lax.broadcasted_iota(jnp.int32, (2 * CH, 256), 1)
    p_half = jnp.where(p_row >= CH, 1, 0)
    p_out = p_row - CH * p_half
    p_owner = (p_out * 43691) >> 18
    p_slot = ((p_owner >> 1) ^ chip) + 8 * ((p_owner & 1) ^ core)
    pick = jnp.where(p_slot * 16 + p_half * 8 + (p_out - 6 * p_owner) == p_col, 1.0, 0.0).astype(BF16)

    def assemble(k):
        for copy in f_copy[k]:
            copy.wait_recv()
        packed = w_buf[k].reshape(256, HALF)
        both = jnp.dot(pick, packed, preferred_element_type=F32).astype(BF16)
        w_full[k, :, :HALF] = both[:CH]
        w_full[k, :, HALF:] = both[CH:]

    def flip(k):
        for a in range(3):
            turned = jnp.transpose(w_full[k, :, (2 - a) * KP : (3 - a) * KP])
            blocks = [turned[(8 - t) * CH : (9 - t) * CH, :] for t in range(9)]
            w_flip[k, :, a * KP : (a + 1) * KP] = jnp.concatenate(
                blocks + [jnp.zeros((CH, KP - KA), BF16)], axis=1
            )

    def convolve(weights, k, which):
        total = None
        for a in range(3):
            part = jnp.dot(
                weights[k, :, a * KP : (a + 1) * KP],
                cols[which, :, a * LT : a * LT + 512],
                preferred_element_type=F32,
            )
            total = part if total is None else total + part
        return total

    one_copy, two_copy, y_copy, z_copy, g_copy = {}, {}, {}, {}, {}

    def start_term(m, which):
        term[m, :, 3 * KP :] = jnp.zeros((64, LT), F32)
        one_copy[m] = []
        for a in range(3):
            part = lax.dot_general(
                gp_buf[m], cols[which, :, a * LT : a * LT + 512],
                (((1,), (1,)), ((), ())), preferred_element_type=F32,
            )
            one_out[m, a] = part[64:].astype(BF16)
            one_copy[m].append(
                send(one_out.at[m, a], one_in.at[m, a], one_send.at[m, a], one_recv.at[m, a], sibling)
            )
            term[m, :, a * KP : (a + 1) * KP] = part[:64]

    def reduce_chips(m):
        for a in range(3):
            one_copy[m][a].wait_recv()
            term[m, :, a * KP : (a + 1) * KP] += one_in[m, a].astype(F32)
        two_copy[m] = []
        for j in range(1, 8):
            two_out[m, j - 1] = jnp.concatenate(
                [term[m, 8 * j : 8 * j + 8, :HALF], term[m, 8 * j : 8 * j + 8, HALF:]], axis=0
            ).astype(BF16)
            two_copy[m].append(
                send(two_out.at[m, j - 1], two_in.at[m, j - 1], two_send.at[m, j - 1],
                     two_recv.at[m, j - 1], chip_mate(j))
            )

    def reduce_rows(m):
        total = jnp.concatenate([term[m, :8, :HALF], term[m, :8, HALF:]], axis=0)
        for j in range(1, 8):
            two_copy[m][j - 1].wait_recv()
            total = total + two_in[m, j - 1].astype(F32)
        tiles = [total[:8, n * LT : (n + 1) * LT] for n in range(11)]
        tiles += [total[8:, n * LT : (n + 1) * LT] for n in range(10)]
        for p in range(7):
            sum_src[m, p] = jnp.concatenate(tiles[3 * p : 3 * p + 3], axis=1)
        sum_src[m, 7] = jnp.zeros((8, 3 * LT), F32)
        y_copy[m] = [
            send(sum_src.at[m, xor(row, j)], sum_in.at[m, j - 1], y_send.at[m, j - 1],
                 y_recv.at[m, j - 1], row_mate(j))
            for j in range(1, 8)
        ]

    def reduce_cols(m):
        total = sum_src[m, row]
        for j in range(1, 8):
            y_copy[m][j - 1].wait_recv()
            total = total + sum_in[m, j - 1]
        piece[m] = total
        z_copy[m] = [
            send(piece.at[m], piece_in.at[m, j - 1], z_send.at[m, j - 1], z_recv.at[m, j - 1], col_mate(j))
            for j in range(1, 4)
        ]

    def share_rows(m):
        for copy in z_copy[m]:
            copy.wait_recv()
        whole[m, row] = (piece[m] + piece_in[m, 0]) + (piece_in[m, 1] + piece_in[m, 2])
        g_copy[m] = [
            send(whole.at[m, row], whole.at[m, row], g_send.at[m, j - 1], g_recv.at[m, j - 1], row_mate(j))
            for j in range(1, 8)
        ]

    def finish(m, out_ref):
        for copy in g_copy[m]:
            copy.wait_recv()
        flat = jnp.concatenate([whole[m, p][:6] for p in range(7)], axis=1)
        out_ref[...] = jnp.concatenate([flat[:, a * KP : a * KP + KA] for a in range(3)], axis=1)

    forward_weight(0)
    unroll_edges(0)
    unroll_edges(1)
    assemble(0)
    hidden = convolve(w_full, 0, 0)
    a_two = []
    for j in range(4):
        norm, scale = normalized(lanes_of(hidden, j))
        n_buf[1, j], r_buf[1, j] = norm, scale
        a_two.append((occupied * (norm * sigmoid(norm))).astype(BF16))
    send_halo(2, a_two[0], a_two[3])
    forward_weight(1)
    unroll_middle(2, a_two)
    unroll_edges(2)

    start_term(1, 2)

    assemble(1)
    flip(1)
    back = convolve(w_flip, 1, 1)
    g_one = []
    for j in range(4):
        inner = act_vjp(n_buf[1, j], r_buf[1, j], occupied * lanes_of(back, j))
        g_one.append((occupied * inner).astype(BF16))
    send_halo(3, g_one[0], g_one[3])
    gp_buf[0] = spread_rows(g_one)
    reduce_chips(1)
    start_term(0, 0)

    unroll_middle(3, g_one)
    branch = convolve(w_full, 1, 2)
    reduce_chips(0)
    reduce_rows(1)
    outs = unpaired([occupied * (x_buf[0, j] + lanes_of(branch, j)) for j in range(4)], low)
    for j in range(4):
        bout_ref[0, 0, :, j * LT : (j + 1) * LT] = outs[j].astype(BF16)
    flip(0)
    reduce_cols(1)
    unroll_edges(3)
    reduce_rows(0)
    back = convolve(w_flip, 0, 3)
    share_rows(1)
    reduce_cols(0)
    outs = []
    for j in range(4):
        inner = act_vjp(n_buf[0, j], r_buf[0, j], occupied * lanes_of(back, j))
        outs.append(occupied * (x_buf[1, j] + inner))
    outs = unpaired(outs, low)
    for j in range(4):
        gin_ref[0, 0, :, j * LT : (j + 1) * LT] = outs[j].astype(BF16)
    share_rows(0)
    finish(1, gtwo_ref)
    finish(0, gone_ref)
    for copy in sent:
        copy.wait_send()


def body(features, w_first, w_second, neighbours, live_counts, output_gradient):
    vmem = pl.BlockSpec(memory_space=pltpu.VMEM)
    smem = pl.BlockSpec(memory_space=pltpu.SMEM)
    dma = pltpu.SemaphoreType.DMA
    return pl.pallas_call(
        kernel,
        out_shape=(
            jax.ShapeDtypeStruct(features.shape, BF16),
            jax.ShapeDtypeStruct(features.shape, BF16),
            jax.ShapeDtypeStruct(w_first.shape, F32),
            jax.ShapeDtypeStruct(w_second.shape, F32),
        ),
        in_specs=[vmem, vmem, vmem, smem, smem, vmem],
        out_specs=(vmem, vmem, vmem, vmem),
        scratch_shapes=[
            pltpu.VMEM((2, 16, 16, HALF), BF16),
            pltpu.VMEM((2, CH, 2 * HALF), BF16),
            pltpu.VMEM((2, CH, 3 * KP), BF16),
            pltpu.VMEM((4, 2, CH, LT), BF16),
            pltpu.VMEM((4, 2, CH, LT), BF16),
            pltpu.VMEM((4, KP, 6 * LT), BF16),
            pltpu.VMEM((2, 4, CH, LT), F32),
            pltpu.VMEM((2, 4, CH, LT), F32),
            pltpu.VMEM((2, 4, 1, LT), F32),
            pltpu.VMEM((2, LT, 512), BF16),
            pltpu.VMEM((2, 64, 2 * HALF), F32),
            pltpu.VMEM((2, 3, 64, KP), BF16),
            pltpu.VMEM((2, 3, 64, KP), BF16),
            pltpu.VMEM((2, 7, 16, HALF), BF16),
            pltpu.VMEM((2, 7, 16, HALF), BF16),
            pltpu.VMEM((2, 8, 8, 3 * LT), F32),
            pltpu.VMEM((2, 7, 8, 3 * LT), F32),
            pltpu.VMEM((2, 8, 3 * LT), F32),
            pltpu.VMEM((2, 3, 8, 3 * LT), F32),
            pltpu.VMEM((2, 8, 8, 3 * LT), F32),
            dma((2, 7)), dma((2, 7)), dma((2, 8)), dma((2, 8)), dma((4, 2)), dma((4, 2)),
            dma((2, 3)), dma((2, 3)), dma((2, 7)), dma((2, 7)), dma((2, 7)), dma((2, 7)),
            dma((2, 3)), dma((2, 3)), dma((2, 7)), dma((2, 7)),
        ],
        compiler_params=pltpu.CompilerParams(
            collective_id=0, has_side_effects=True, vmem_limit_bytes=48 * 1024 * 1024
        ),
    )(features, w_first, w_second, neighbours, live_counts, output_gradient)


def solution(mesh):
    blocks = P("fsdp", "space", None, None)
    weights = P("fsdp", None)
    return jax.shard_map(
        body,
        mesh=mesh,
        in_specs=(blocks, weights, weights, P("fsdp", "space", None), P("fsdp", "space"), blocks),
        out_specs=(blocks, blocks, weights, weights),
        check_vma=False,
    )
```

time: 650 us -> 73.6 us (0.11)
  the two profiles are of different devices: /device:TPU:4 before, /device:TPU:2 now
where the time goes in v1:
time: 73.6 us; the launch traced here: 73.3 us
  Pallas kernels  66.1 us (90%)
  local copies, waits for them, and re-layouts  5.9 us (8%)
  between operations  1.33 us (2%)
    pallas_call x1, Pallas kernels, body(): pl.pallas_call(kernel, out_shape=(jax.ShapeDtypeStruct(features.shape, BF...  66.1 us
    unnamed x14, local copies, waits for them, and re-layouts  5.9 us

profile of v1, /device:TPU:2, one launch (start us, length us, event | category | flops | bytes accessed | tf_op | source)
XLA Modules:
  0.0 73.3 jit_solution(8683851185587104554)
XLA Ops:
  0.6 0.0 copy-start.4
  1.3 0.0 copy-done.4
  1.3 0.0 copy-start
  1.3 0.9 %copy-done = bf16[1,1,96,512]{3,2,1,0:T(8,128)(2,1)S(1)} copy-done((bf16[1,1,96,512]{3,2,1,0:T(8,128)(2,1)S(1)}, bf16[1,1,96,512]{3,2,1,0:T(8,128)(2,1)}, u32[]{:S(2)}) %copy-start) | copy-done | bytes 98328
  2.2 0.0 copy-start.1
  2.2 0.9 %copy-done.1 = bf16[1,1,96,512]{3,2,1,0:T(8,128)(2,1)S(1)} copy-done((bf16[1,1,96,512]{3,2,1,0:T(8,128)(2,1)S(1)}, bf16[1,1,96,512]{3,2,1,0:T(8,128)(2,1)}, u32[]{:S(2)}) %copy-start.1) | copy-done | bytes 98328
  3.1 0.0 copy-start.2
  3.1 0.8 %copy-done.2 = bf16[6,2592]{1,0:T(8,128)(2,1)S(1)} copy-done((bf16[6,2592]{1,0:T(8,128)(2,1)S(1)}, bf16[6,2592]{1,0:T(8,128)(2,1)}, u32[]{:S(2)}) %copy-start.2) | copy-done | bytes 31128
  3.9 0.0 copy-start.3
  3.9 0.8 %copy-done.3 = bf16[6,2592]{1,0:T(8,128)(2,1)S(1)} copy-done((bf16[6,2592]{1,0:T(8,128)(2,1)S(1)}, bf16[6,2592]{1,0:T(8,128)(2,1)}, u32[]{:S(2)}) %copy-start.3) | copy-done | bytes 31128
  4.7 66.1 %shard_map.93 = (bf16[1,1,96,512]{3,2,1,0:T(8,128)(2,1)S(1)}, bf16[1,1,96,512]{3,2,1,0:T(8,128)(2,1)S(1)}, f32[6,2592]{1,0:T(8,128)S(1)}, f32[6,2592]{1,0:T(8,128)S(1)}) custom-call(bf16[1,1,96,512]{3,2,1,0:T(8,128)(2,1)S(1)} %copy-done, bf16[6,2592]{1,0:T(8,128)(2,1)S(1)} %copy-done.2, bf16[6,2592]{1,0:T(8,128)(2,1)S(1)} %copy-done.3, ...), custom_call_target="tpu_custom_call" | custom-call | tf_op jit(solution)/shard_map/pallas_call | solution.py:425
  70.8 0.6 copy.15
  71.4 0.6 copy.16
  72.0 0.6 copy.17
  72.7 0.6 copy.18
Async XLA Ops:
  0.6 0.7 copy-start.4
  1.3 0.9 %copy-start = (bf16[1,1,96,512]{3,2,1,0:T(8,128)(2,1)S(1)}, bf16[1,1,96,512]{3,2,1,0:T(8,128)(2,1)}, u32[]{:S(2)}) copy-start(bf16[1,1,96,512]{3,2,1,0:T(8,128)(2,1)} %feat_ref.1) | copy-start | bytes 294916
  2.2 0.9 %copy-start.1 = (bf16[1,1,96,512]{3,2,1,0:T(8,128)(2,1)S(1)}, bf16[1,1,96,512]{3,2,1,0:T(8,128)(2,1)}, u32[]{:S(2)}) copy-start(bf16[1,1,96,512]{3,2,1,0:T(8,128)(2,1)} %grad_ref.1) | copy-start | bytes 294916
  3.1 0.8 %copy-start.2 = (bf16[6,2592]{1,0:T(8,128)(2,1)S(1)}, bf16[6,2592]{1,0:T(8,128)(2,1)}, u32[]{:S(2)}) copy-start(bf16[6,2592]{1,0:T(8,128)(2,1)} %wone_ref.1) | copy-start | bytes 93316
  3.9 0.8 %copy-start.3 = (bf16[6,2592]{1,0:T(8,128)(2,1)S(1)}, bf16[6,2592]{1,0:T(8,128)(2,1)}, u32[]{:S(2)}) copy-start(bf16[6,2592]{1,0:T(8,128)(2,1)} %wtwo_ref.1) | copy-start | bytes 93316

commit v2 on v1

--- a/solution.py
+++ b/solution.py
@@ -15,6 +15,7 @@
 KP = 896
 HALF = 11 * LT
 EPS = 1e-05
+FAR_FIRST = (6, 2, 7, 5, 3, 1, 4)
 
 
 def xor(value, pattern):
@@ -69,13 +70,23 @@
 
 
 def kernel(
-    feat_ref, wone_ref, wtwo_ref, near_ref, live_ref, grad_ref,
-    bout_ref, gin_ref, gone_ref, gtwo_ref,
+    feat_hbm, wone_hbm, wtwo_hbm, near_hbm, live_hbm, grad_hbm,
+    bout_hbm, gin_hbm, gone_hbm, gtwo_hbm,
+    bout_ref, gin_ref, gone_ref, gtwo_ref, feat_ref, wone_ref, wtwo_ref, near_ref, live_ref, grad_ref, load_sem, save_sem,
     w_buf, w_full, w_flip, halo_out, halo_in, cols, x_buf, n_buf, r_buf, gp_buf,
     term, one_out, one_in, two_out, two_in, sum_src, sum_in, piece, piece_in, whole,
     w_send, w_recv, f_send, f_recv, halo_send, halo_recv,
     one_send, one_recv, two_send, two_recv, y_send, y_recv, z_send, z_recv, g_send, g_recv,
 ):
+    loads = [
+        pltpu.make_async_copy(src, dst, load_sem.at[i])
+        for i, (src, dst) in enumerate((
+            (wone_hbm, wone_ref), (wtwo_hbm, wtwo_ref), (feat_hbm, feat_ref),
+            (near_hbm, near_ref), (live_hbm, live_ref), (grad_hbm, grad_ref),
+        ))
+    ]
+    for copy in loads:
+        copy.start()
     fsdp = lax.axis_index("fsdp")
     space = lax.axis_index("space")
     chip, core = lax.div(fsdp, 2), lax.rem(fsdp, 2)
@@ -106,6 +117,13 @@
 
     sent = []
 
+    saves = [
+        pltpu.make_async_copy(src, dst, save_sem.at[i])
+        for i, (src, dst) in enumerate((
+            (bout_ref, bout_hbm), (gin_ref, gin_hbm), (gone_ref, gone_hbm), (gtwo_ref, gtwo_hbm),
+        ))
+    ]
+
     def send(src, dst, send_sem, recv_sem, device):
         copy = pltpu.make_async_remote_copy(
             src_ref=src, dst_ref=dst, send_sem=send_sem, recv_sem=recv_sem,
@@ -116,6 +134,7 @@
         return copy
 
     for k, ref in enumerate((wone_ref, wtwo_ref)):
+        loads[k].wait()
         rows = ref[...].astype(F32)
         gap = jnp.zeros((6, KP - KA), F32)
         parts = []
@@ -131,17 +150,20 @@
     for k in range(2):
         own = [send(w_buf.at[k, 0], w_buf.at[k, 8], f_send.at[k, 0], f_recv.at[k, 0], sibling)]
         f_copy.append(own)
-        w_copy.append([
-            send(w_buf.at[k, 0], w_buf.at[k, j], w_send.at[k, j - 1], w_recv.at[k, j - 1], chip_mate(j))
-            for j in range(1, 8)
-        ])
+        w_copy.append({
+            j: send(w_buf.at[k, 0], w_buf.at[k, j], w_send.at[k, j - 1], w_recv.at[k, j - 1], chip_mate(j))
+            for j in FAR_FIRST
+        })
 
     def forward_weight(k):
-        for j in range(1, 8):
-            w_copy[k][j - 1].wait_recv()
+        for j in reversed(FAR_FIRST):
+            w_copy[k][j].wait_recv()
             f_copy[k].append(
                 send(w_buf.at[k, j], w_buf.at[k, 8 + j], f_send.at[k, j], f_recv.at[k, j], sibling)
             )
+
+    for copy in loads[2:]:
+        copy.wait()
 
     lane = lax.broadcasted_iota(jnp.int32, (1, LT), 1)
     z_pos, y_pos = lane & 7, (lane >> 3) & 7
@@ -309,20 +331,20 @@
         for a in range(3):
             one_copy[m][a].wait_recv()
             term[m, :, a * KP : (a + 1) * KP] += one_in[m, a].astype(F32)
-        two_copy[m] = []
-        for j in range(1, 8):
+        two_copy[m] = {}
+        for j in FAR_FIRST:
             two_out[m, j - 1] = jnp.concatenate(
                 [term[m, 8 * j : 8 * j + 8, :HALF], term[m, 8 * j : 8 * j + 8, HALF:]], axis=0
             ).astype(BF16)
-            two_copy[m].append(
-                send(two_out.at[m, j - 1], two_in.at[m, j - 1], two_send.at[m, j - 1],
-                     two_recv.at[m, j - 1], chip_mate(j))
+            two_copy[m][j] = send(
+                two_out.at[m, j - 1], two_in.at[m, j - 1], two_send.at[m, j - 1],
+                two_recv.at[m, j - 1], chip_mate(j),
             )
 
     def reduce_rows(m):
         total = jnp.concatenate([term[m, :8, :HALF], term[m, :8, HALF:]], axis=0)
-        for j in range(1, 8):
-            two_copy[m][j - 1].wait_recv()
+        for j in reversed(FAR_FIRST):
+            two_copy[m][j].wait_recv()
             total = total + two_in[m, j - 1].astype(F32)
         tiles = [total[:8, n * LT : (n + 1) * LT] for n in range(11)]
         tiles += [total[8:, n * LT : (n + 1) * LT] for n in range(10)]
@@ -361,23 +383,22 @@
         flat = jnp.concatenate([whole[m, p][:6] for p in range(7)], axis=1)
         out_ref[...] = jnp.concatenate([flat[:, a * KP : a * KP + KA] for a in range(3)], axis=1)
 
-    forward_weight(0)
+    def silu_tiles(hidden):
+        tiles = []
+        for j in range(4):
+            norm, scale = normalized(lanes_of(hidden, j))
+            n_buf[1, j], r_buf[1, j] = norm, scale
+            tiles.append((occupied * (norm * sigmoid(norm))).astype(BF16))
+        return tiles
+
     unroll_edges(0)
     unroll_edges(1)
+    forward_weight(0)
     assemble(0)
-    hidden = convolve(w_full, 0, 0)
-    a_two = []
-    for j in range(4):
-        norm, scale = normalized(lanes_of(hidden, j))
-        n_buf[1, j], r_buf[1, j] = norm, scale
-        a_two.append((occupied * (norm * sigmoid(norm))).astype(BF16))
+    a_two = silu_tiles(convolve(w_full, 0, 0))
     send_halo(2, a_two[0], a_two[3])
     forward_weight(1)
     unroll_middle(2, a_two)
-    unroll_edges(2)
-
-    start_term(1, 2)
-
     assemble(1)
     flip(1)
     back = convolve(w_flip, 1, 1)
@@ -387,23 +408,25 @@
         g_one.append((occupied * inner).astype(BF16))
     send_halo(3, g_one[0], g_one[3])
     gp_buf[0] = spread_rows(g_one)
+    start_term(0, 0)
+    unroll_edges(2)
+    start_term(1, 2)
+    reduce_chips(0)
     reduce_chips(1)
-    start_term(0, 0)
 
     unroll_middle(3, g_one)
     branch = convolve(w_full, 1, 2)
-    reduce_chips(0)
-    reduce_rows(1)
     outs = unpaired([occupied * (x_buf[0, j] + lanes_of(branch, j)) for j in range(4)], low)
     for j in range(4):
         bout_ref[0, 0, :, j * LT : (j + 1) * LT] = outs[j].astype(BF16)
+    saves[0].start()
     flip(0)
+    reduce_rows(0)
+    reduce_rows(1)
+    unroll_edges(3)
+    back = convolve(w_flip, 0, 3)
+    reduce_cols(0)
     reduce_cols(1)
-    unroll_edges(3)
-    reduce_rows(0)
-    back = convolve(w_flip, 0, 3)
-    share_rows(1)
-    reduce_cols(0)
     outs = []
     for j in range(4):
         inner = act_vjp(n_buf[0, j], r_buf[0, j], occupied * lanes_of(back, j))
@@ -411,18 +434,32 @@
     outs = unpaired(outs, low)
     for j in range(4):
         gin_ref[0, 0, :, j * LT : (j + 1) * LT] = outs[j].astype(BF16)
+    saves[1].start()
     share_rows(0)
+    share_rows(1)
+    finish(0, gone_ref)
+    saves[2].start()
     finish(1, gtwo_ref)
-    finish(0, gone_ref)
+    saves[3].start()
     for copy in sent:
         copy.wait_send()
+    for copy in saves:
+        copy.wait()
+
+
+def store(*refs):
+    copies = [pltpu.make_async_copy(refs[i], refs[4 + i], refs[8].at[i]) for i in range(4)]
+    for copy in copies:
+        copy.start()
+    for copy in copies:
+        copy.wait()
 
 
 def body(features, w_first, w_second, neighbours, live_counts, output_gradient):
+    dma = pltpu.SemaphoreType.DMA
     vmem = pl.BlockSpec(memory_space=pltpu.VMEM)
-    smem = pl.BlockSpec(memory_space=pltpu.SMEM)
-    dma = pltpu.SemaphoreType.DMA
-    return pl.pallas_call(
+    hbm = pl.BlockSpec(memory_space=pltpu.HBM)
+    results = pl.pallas_call(
         kernel,
         out_shape=(
             jax.ShapeDtypeStruct(features.shape, BF16),
@@ -430,9 +467,21 @@
             jax.ShapeDtypeStruct(w_first.shape, F32),
             jax.ShapeDtypeStruct(w_second.shape, F32),
         ),
-        in_specs=[vmem, vmem, vmem, smem, smem, vmem],
-        out_specs=(vmem, vmem, vmem, vmem),
+        in_specs=[hbm] * 6,
+        out_specs=(hbm,) * 4,
         scratch_shapes=[
+            pltpu.VMEM(features.shape, BF16),
+            pltpu.VMEM(features.shape, BF16),
+            pltpu.VMEM(w_first.shape, F32),
+            pltpu.VMEM(w_second.shape, F32),
+            pltpu.VMEM(features.shape, BF16),
+            pltpu.VMEM(w_first.shape, BF16),
+            pltpu.VMEM(w_second.shape, BF16),
+            pltpu.SMEM(neighbours.shape, jnp.int32),
+            pltpu.SMEM(live_counts.shape, jnp.int32),
+            pltpu.VMEM(features.shape, BF16),
+            dma((6,)),
+            dma((4,)),
             pltpu.VMEM((2, 16, 16, HALF), BF16),
             pltpu.VMEM((2, CH, 2 * HALF), BF16),
             pltpu.VMEM((2, CH, 3 * KP), BF16),
@@ -458,9 +507,17 @@
             dma((2, 3)), dma((2, 3)), dma((2, 7)), dma((2, 7)),
         ],
         compiler_params=pltpu.CompilerParams(
-            collective_id=0, has_side_effects=True, vmem_limit_bytes=48 * 1024 * 1024
+            collective_id=0, has_side_effects=True, vmem_limit_bytes=63 * 1024 * 1024
         ),
     )(features, w_first, w_second, neighbours, live_counts, output_gradient)
+    return pl.pallas_call(
+        store,
+        out_shape=tuple(jax.ShapeDtypeStruct(r.shape, r.dtype) for r in results),
+        in_specs=[vmem] * 4,
+        out_specs=(hbm,) * 4,
+        scratch_shapes=[dma((4,))],
+        compiler_params=pltpu.CompilerParams(vmem_limit_bytes=63 * 1024 * 1024),
+    )(*results)
 
 
 def solution(mesh):

time: 73.6 us -> 65.6 us (0.89)
  the two profiles are of different devices: /device:TPU:2 before, /device:TPU:8 now
where the time goes in v2:
time: 65.6 us; the launch traced here: 65.4 us
  Pallas kernels  64.1 us (98%)
  between operations  1.29 us (2%)
    pallas_call x1, Pallas kernels, body(): pl.pallas_call(kernel, out_shape=(jax.ShapeDtypeStruct(features.shape, BF...  62.3 us
    pallas_call x1, Pallas kernels, body(): pl.pallas_call(store, out_shape=tuple((jax.ShapeDtypeStruct(r.shape, r.dt...  1.79 us

profile of v2, /device:TPU:8, one launch (start us, length us, event | category | flops | bytes accessed | tf_op | source)
XLA Modules:
  0.0 65.4 jit_solution(12556985562460952874)
XLA Ops:
  1.3 62.3 %shard_map.93 = (bf16[1,1,96,512]{3,2,1,0:T(8,128)(2,1)}, bf16[1,1,96,512]{3,2,1,0:T(8,128)(2,1)}, f32[6,2592]{1,0:T(8,128)}, f32[6,2592]{1,0:T(8,128)}) custom-call(bf16[1,1,96,512]{3,2,1,0:T(8,128)(2,1)} %feat_hbm.1, bf16[6,2592]{1,0:T(8,128)(2,1)} %wone_hbm.1, bf16[6,2592]{1,0:T(8,128)(2,1)} %wtwo_hbm.1, s32[1,1,6]{2,1,0:T(1,128)} %near_hbm.1, ...), custom_call_target="tpu_custom_call" | custom-call | tf_op jit(solution)/shard_map/pallas_call | solution.py:462
  63.6 1.8 %shard_map.94 = (bf16[1,1,96,512]{3,2,1,0:T(8,128)(2,1)}, bf16[1,1,96,512]{3,2,1,0:T(8,128)(2,1)}, f32[6,2592]{1,0:T(8,128)}, f32[6,2592]{1,0:T(8,128)}) custom-call(bf16[1,1,96,512]{3,2,1,0:T(8,128)(2,1)} %get-tuple-element.8.refs_0_, bf16[1,1,96,512]{3,2,1,0:T(8,128)(2,1)} %get-tuple-element.9.refs_1_, f32[6,2592]{1,0:T(8,128)} %get-tuple-element.10.refs_2_, ...), custom_call_target="tpu_custom_call" | custom-call | tf_op jit(solution)/shard_map/pallas_call | solution.py:513

commit v3 on v2

--- a/solution.py
+++ b/solution.py
@@ -15,6 +15,7 @@
 KP = 896
 HALF = 11 * LT
 EPS = 1e-05
+WHOLE = BF16
 FAR_FIRST = (6, 2, 7, 5, 3, 1, 4)
 
 
@@ -73,8 +74,8 @@
     feat_hbm, wone_hbm, wtwo_hbm, near_hbm, live_hbm, grad_hbm,
     bout_hbm, gin_hbm, gone_hbm, gtwo_hbm,
     bout_ref, gin_ref, gone_ref, gtwo_ref, feat_ref, wone_ref, wtwo_ref, near_ref, live_ref, grad_ref, load_sem, save_sem,
-    w_buf, w_full, w_flip, halo_out, halo_in, cols, x_buf, n_buf, r_buf, gp_buf,
-    term, one_out, one_in, two_out, two_in, sum_src, sum_in, piece, piece_in, whole,
+    w_buf, w_full, w_flip, halo_out, halo_in, cols, x_buf, n_buf, r_buf, gp_buf, gp_wide,
+    term, one_out, one_in, two_out, two_in, own_sum, sum_src, sum_in, piece, piece_in, whole,
     w_send, w_recv, f_send, f_recv, halo_send, halo_recv,
     one_send, one_recv, two_send, two_recv, y_send, y_recv, z_send, z_recv, g_send, g_recv,
 ):
@@ -183,7 +184,7 @@
     def wide(mask):
         return jnp.broadcast_to(mask, (CH, LT)).astype(BF16)
 
-    inside = {"low": high_f, "mid": jnp.ones((1, LT), F32), "high": low_f}
+    inside = {"low": high_f, "mid": jnp.ones((1, LT), F32), "high": low_f, "edge": jnp.zeros((1, LT), F32)}
     z_keep = {c: wide(in_z[c]) for c in (0, 2)}
     y_keep = {b: wide(in_y[b]) for b in (0, 2)}
     z_wrap = {
@@ -196,8 +197,8 @@
             for c in range(3):
                 y_wrap[b, c, w] = wide(base if c == 1 else base * in_z[c])
 
-    def unroll_tile(which, j, tile):
-        w = "low" if j == 0 else "high" if j == 5 else "mid"
+    def unroll_tile(which, j, tile, w=None):
+        w = w or ("low" if j == 0 else "high" if j == 5 else "mid")
         for c in range(3):
             if c == 1:
                 along = tile
@@ -274,8 +275,6 @@
         whole_g = jnp.concatenate(list(tiles), axis=1)
         return jnp.dot(spread, whole_g, preferred_element_type=F32).astype(BF16)
 
-    gp_buf[1] = spread_rows(g_two)
-
     p_row = lax.broadcasted_iota(jnp.int32, (2 * CH, 256), 0)
     p_col = lax.broadcasted_iota(jnp.int32, (2 * CH, 256), 1)
     p_half = jnp.where(p_row >= CH, 1, 0)
@@ -311,14 +310,25 @@
             total = part if total is None else total + part
         return total
 
-    one_copy, two_copy, y_copy, z_copy, g_copy = {}, {}, {}, {}, {}
-
-    def start_term(m, which):
+    one_copy, two_copy = {}, {}
+
+    def first_pair(a):
+        return gp_buf[...], cols[0, :, a * LT : a * LT + 512]
+
+    def second_pair(a):
+        if a == 0:
+            return gp_wide[:, 2 * LT : 7 * LT], cols[2, :, LT : 6 * LT]
+        if a == 1:
+            return gp_wide[:, LT : 5 * LT], cols[2, :, LT : 5 * LT]
+        left = jnp.concatenate([gp_wide[:, : 4 * LT], gp_wide[:, 7 * LT :]], axis=1)
+        return left, cols[2, :, LT : 6 * LT]
+
+    def start_term(m, pair):
         term[m, :, 3 * KP :] = jnp.zeros((64, LT), F32)
         one_copy[m] = []
         for a in range(3):
             part = lax.dot_general(
-                gp_buf[m], cols[which, :, a * LT : a * LT + 512],
+                *pair(a),
                 (((1,), (1,)), ((), ())), preferred_element_type=F32,
             )
             one_out[m, a] = part[64:].astype(BF16)
@@ -341,47 +351,62 @@
                 two_recv.at[m, j - 1], chip_mate(j),
             )
 
-    def reduce_rows(m):
+    def sum_chips(m):
         total = jnp.concatenate([term[m, :8, :HALF], term[m, :8, HALF:]], axis=0)
         for j in reversed(FAR_FIRST):
             two_copy[m][j].wait_recv()
             total = total + two_in[m, j - 1].astype(F32)
         tiles = [total[:8, n * LT : (n + 1) * LT] for n in range(11)]
-        tiles += [total[8:, n * LT : (n + 1) * LT] for n in range(10)]
+        return tiles + [total[8:, n * LT : (n + 1) * LT] for n in range(10)]
+
+    rows_far_first = (4, 5, 3, 2, 6, 7, 1)
+    later = {}
+
+    def reduce_rows():
+        other = sum_chips(1)
+        both = [sum_chips(0), other]
         for p in range(7):
-            sum_src[m, p] = jnp.concatenate(tiles[3 * p : 3 * p + 3], axis=1)
-        sum_src[m, 7] = jnp.zeros((8, 3 * LT), F32)
-        y_copy[m] = [
-            send(sum_src.at[m, xor(row, j)], sum_in.at[m, j - 1], y_send.at[m, j - 1],
-                 y_recv.at[m, j - 1], row_mate(j))
-            for j in range(1, 8)
+            joined = jnp.concatenate(
+                [jnp.concatenate(tiles[3 * p : 3 * p + 3], axis=1) for tiles in both], axis=0
+            )
+            own_sum[p] = joined
+            sum_src[p] = joined.astype(BF16)
+        own_sum[7] = jnp.zeros((16, 3 * LT), F32)
+        sum_src[7] = jnp.zeros((16, 3 * LT), BF16)
+        later["y"] = [
+            send(sum_src.at[xor(row, j)], sum_in.at[j - 1], y_send.at[j - 1], y_recv.at[j - 1], row_mate(j))
+            for j in rows_far_first
         ]
 
-    def reduce_cols(m):
-        total = sum_src[m, row]
-        for j in range(1, 8):
-            y_copy[m][j - 1].wait_recv()
-            total = total + sum_in[m, j - 1]
-        piece[m] = total
-        z_copy[m] = [
-            send(piece.at[m], piece_in.at[m, j - 1], z_send.at[m, j - 1], z_recv.at[m, j - 1], col_mate(j))
-            for j in range(1, 4)
+    def reduce_cols():
+        for copy in later["y"]:
+            copy.wait_recv()
+        total = own_sum[row]
+        for j in range(7):
+            total = total + sum_in[j].astype(F32)
+        piece[...] = total.astype(BF16)
+        later["z"] = [
+            send(piece, piece_in.at[j - 1], z_send.at[j - 1], z_recv.at[j - 1], col_mate(j))
+            for j in (2, 3, 1)
         ]
 
-    def share_rows(m):
-        for copy in z_copy[m]:
+    def share_rows():
+        for copy in later["z"]:
             copy.wait_recv()
-        whole[m, row] = (piece[m] + piece_in[m, 0]) + (piece_in[m, 1] + piece_in[m, 2])
-        g_copy[m] = [
-            send(whole.at[m, row], whole.at[m, row], g_send.at[m, j - 1], g_recv.at[m, j - 1], row_mate(j))
-            for j in range(1, 8)
+        parts = [piece[...].astype(F32)] + [piece_in[j].astype(F32) for j in range(3)]
+        whole[row] = ((parts[0] + parts[1]) + (parts[2] + parts[3])).astype(WHOLE)
+        later["g"] = [
+            send(whole.at[row], whole.at[row], g_send.at[j - 1], g_recv.at[j - 1], row_mate(j))
+            for j in rows_far_first
         ]
 
-    def finish(m, out_ref):
-        for copy in g_copy[m]:
+    def finish():
+        for copy in later["g"]:
             copy.wait_recv()
-        flat = jnp.concatenate([whole[m, p][:6] for p in range(7)], axis=1)
-        out_ref[...] = jnp.concatenate([flat[:, a * KP : a * KP + KA] for a in range(3)], axis=1)
+        pieces = [whole[p].astype(F32) for p in range(7)]
+        for m, out_ref in enumerate((gone_ref, gtwo_ref)):
+            flat = jnp.concatenate([one[8 * m : 8 * m + 6] for one in pieces], axis=1)
+            out_ref[...] = jnp.concatenate([flat[:, a * KP : a * KP + KA] for a in range(3)], axis=1)
 
     def silu_tiles(hidden):
         tiles = []
@@ -393,12 +418,18 @@
 
     unroll_edges(0)
     unroll_edges(1)
+    gp_wide[...] = spread_rows(
+        [halo_out[1, 1] * wide(high_f)] + g_two + [halo_out[1, 0] * wide(low_f)]
+        + [halo_in[1, 0] * wide(high_f * named(1)), halo_in[1, 1] * wide(low_f * named(0))]
+    )
     forward_weight(0)
+    forward_weight(1)
     assemble(0)
     a_two = silu_tiles(convolve(w_full, 0, 0))
     send_halo(2, a_two[0], a_two[3])
-    forward_weight(1)
     unroll_middle(2, a_two)
+    unroll_tile(2, 5, a_two[0] * wide(low_f) + a_two[3] * wide(high_f), "edge")
+    start_term(1, second_pair)
     assemble(1)
     flip(1)
     back = convolve(w_flip, 1, 1)
@@ -407,12 +438,11 @@
         inner = act_vjp(n_buf[1, j], r_buf[1, j], occupied * lanes_of(back, j))
         g_one.append((occupied * inner).astype(BF16))
     send_halo(3, g_one[0], g_one[3])
-    gp_buf[0] = spread_rows(g_one)
-    start_term(0, 0)
+    gp_buf[...] = spread_rows(g_one)
+    start_term(0, first_pair)
+    reduce_chips(1)
+    reduce_chips(0)
     unroll_edges(2)
-    start_term(1, 2)
-    reduce_chips(0)
-    reduce_chips(1)
 
     unroll_middle(3, g_one)
     branch = convolve(w_full, 1, 2)
@@ -421,12 +451,10 @@
         bout_ref[0, 0, :, j * LT : (j + 1) * LT] = outs[j].astype(BF16)
     saves[0].start()
     flip(0)
-    reduce_rows(0)
-    reduce_rows(1)
+    reduce_rows()
     unroll_edges(3)
     back = convolve(w_flip, 0, 3)
-    reduce_cols(0)
-    reduce_cols(1)
+    reduce_cols()
     outs = []
     for j in range(4):
         inner = act_vjp(n_buf[0, j], r_buf[0, j], occupied * lanes_of(back, j))
@@ -435,11 +463,9 @@
     for j in range(4):
         gin_ref[0, 0, :, j * LT : (j + 1) * LT] = outs[j].astype(BF16)
     saves[1].start()
-    share_rows(0)
-    share_rows(1)
-    finish(0, gone_ref)
+    share_rows()
+    finish()
     saves[2].start()
-    finish(1, gtwo_ref)
     saves[3].start()
     for copy in sent:
         copy.wait_send()
@@ -491,20 +517,22 @@
             pltpu.VMEM((2, 4, CH, LT), F32),
             pltpu.VMEM((2, 4, CH, LT), F32),
             pltpu.VMEM((2, 4, 1, LT), F32),
-            pltpu.VMEM((2, LT, 512), BF16),
+            pltpu.VMEM((LT, 512), BF16),
+            pltpu.VMEM((LT, 8 * LT), BF16),
             pltpu.VMEM((2, 64, 2 * HALF), F32),
             pltpu.VMEM((2, 3, 64, KP), BF16),
             pltpu.VMEM((2, 3, 64, KP), BF16),
             pltpu.VMEM((2, 7, 16, HALF), BF16),
             pltpu.VMEM((2, 7, 16, HALF), BF16),
-            pltpu.VMEM((2, 8, 8, 3 * LT), F32),
-            pltpu.VMEM((2, 7, 8, 3 * LT), F32),
-            pltpu.VMEM((2, 8, 3 * LT), F32),
-            pltpu.VMEM((2, 3, 8, 3 * LT), F32),
-            pltpu.VMEM((2, 8, 8, 3 * LT), F32),
+            pltpu.VMEM((8, 16, 3 * LT), F32),
+            pltpu.VMEM((8, 16, 3 * LT), BF16),
+            pltpu.VMEM((7, 16, 3 * LT), BF16),
+            pltpu.VMEM((16, 3 * LT), BF16),
+            pltpu.VMEM((3, 16, 3 * LT), BF16),
+            pltpu.VMEM((8, 16, 3 * LT), WHOLE),
             dma((2, 7)), dma((2, 7)), dma((2, 8)), dma((2, 8)), dma((4, 2)), dma((4, 2)),
-            dma((2, 3)), dma((2, 3)), dma((2, 7)), dma((2, 7)), dma((2, 7)), dma((2, 7)),
-            dma((2, 3)), dma((2, 3)), dma((2, 7)), dma((2, 7)),
+            dma((2, 3)), dma((2, 3)), dma((2, 7)), dma((2, 7)), dma((7,)), dma((7,)),
+            dma((3,)), dma((3,)), dma((7,)), dma((7,)),
         ],
         compiler_params=pltpu.CompilerParams(
             collective_id=0, has_side_effects=True, vmem_limit_bytes=63 * 1024 * 1024

time: 65.6 us -> 62.3 us (0.950)
  Pallas kernels: 64.1 us -> 60.8 us
    pallas_call x1, Pallas kernels: 62.3 us -> 59.1 us  [body(): pl.pallas_call(kernel, out_shape=(jax.ShapeDtypeStruct(features.shape, BF...]
where the time goes in v3:
time: 62.3 us; the launch traced here: 62.1 us
  Pallas kernels  60.8 us (98%)
  between operations  1.29 us (2%)
    pallas_call x1, Pallas kernels, body(): pl.pallas_call(kernel, out_shape=(jax.ShapeDtypeStruct(features.shape, BF...  59.1 us
    pallas_call x1, Pallas kernels, body(): pl.pallas_call(store, out_shape=tuple((jax.ShapeDtypeStruct(r.shape, r.dt...  1.79 us

profile of v3, /device:TPU:8, one launch (start us, length us, event | category | flops | bytes accessed | tf_op | source)
XLA Modules:
  0.0 62.1 jit_solution(13358449489643019385)
XLA Ops:
  1.3 59.1 %shard_map.93 = (bf16[1,1,96,512]{3,2,1,0:T(8,128)(2,1)}, bf16[1,1,96,512]{3,2,1,0:T(8,128)(2,1)}, f32[6,2592]{1,0:T(8,128)}, f32[6,2592]{1,0:T(8,128)}) custom-call(bf16[1,1,96,512]{3,2,1,0:T(8,128)(2,1)} %feat_hbm.1, bf16[6,2592]{1,0:T(8,128)(2,1)} %wone_hbm.1, bf16[6,2592]{1,0:T(8,128)(2,1)} %wtwo_hbm.1, s32[1,1,6]{2,1,0:T(1,128)} %near_hbm.1, ...), custom_call_target="tpu_custom_call" | custom-call | tf_op jit(solution)/shard_map/pallas_call | solution.py:488
  60.3 1.8 %shard_map.94 = (bf16[1,1,96,512]{3,2,1,0:T(8,128)(2,1)}, bf16[1,1,96,512]{3,2,1,0:T(8,128)(2,1)}, f32[6,2592]{1,0:T(8,128)}, f32[6,2592]{1,0:T(8,128)}) custom-call(bf16[1,1,96,512]{3,2,1,0:T(8,128)(2,1)} %get-tuple-element.8.refs_0_, bf16[1,1,96,512]{3,2,1,0:T(8,128)(2,1)} %get-tuple-element.9.refs_1_, f32[6,2592]{1,0:T(8,128)} %get-tuple-element.10.refs_2_, ...), custom_call_target="tpu_custom_call" | custom-call | tf_op jit(solution)/shard_map/pallas_call | solution.py:541

commit v4 on v3

--- a/solution.py
+++ b/solution.py
@@ -13,7 +13,6 @@
 LT = 128
 KA = 9 * CH
 KP = 896
-HALF = 11 * LT
 EPS = 1e-05
 WHOLE = BF16
 FAR_FIRST = (6, 2, 7, 5, 3, 1, 4)
@@ -48,6 +47,33 @@
         jnp.where(low, half_turn(p0), p1),
         jnp.where(low, half_turn(p2), p3),
     )
+
+
+def packed(rows):
+    tail = [rows[:, n * LT : (n + 1) * LT] for n in range(16, 21)]
+    blank = jnp.zeros((2, LT), rows.dtype)
+    spare = jnp.concatenate(
+        [
+            jnp.concatenate([tail[0][4:6], tail[2][4:6], tail[4][4:6]], axis=1),
+            jnp.concatenate([tail[1][4:6], tail[3][4:6], blank], axis=1),
+        ],
+        axis=0,
+    )
+    last = jnp.concatenate([rows[:4, 16 * LT :], spare], axis=1)
+    return jnp.concatenate([rows[:, : 8 * LT], rows[:, 8 * LT : 16 * LT], last], axis=0)
+
+
+def unpacked(block):
+    tiles = [block[:6, n * LT : (n + 1) * LT] for n in range(8)]
+    tiles += [block[6:12, n * LT : (n + 1) * LT] for n in range(8)]
+    for n in range(5):
+        top, col = 12 + 2 * (n % 2), 5 + n // 2
+        tiles.append(
+            jnp.concatenate(
+                [block[12:16, n * LT : (n + 1) * LT], block[top : top + 2, col * LT : (col + 1) * LT]], axis=0
+            )
+        )
+    return tiles
 
 
 def normalized(u):
@@ -141,9 +167,7 @@
         parts = []
         for a in range(3):
             parts += [rows[:, a * KA : (a + 1) * KA], gap]
-        flat = jnp.concatenate(parts + [jnp.zeros((6, LT), F32)], axis=1)
-        flat = jnp.concatenate([flat, jnp.zeros((2, 2 * HALF), F32)], axis=0)
-        w_buf[k, 0] = jnp.concatenate([flat[:, :HALF], flat[:, HALF:]], axis=0).astype(BF16)
+        w_buf[k, 0] = packed(jnp.concatenate(parts, axis=1)).astype(BF16)
 
     pl.semaphore_wait(barrier, len(mates))
 
@@ -275,21 +299,35 @@
         whole_g = jnp.concatenate(list(tiles), axis=1)
         return jnp.dot(spread, whole_g, preferred_element_type=F32).astype(BF16)
 
-    p_row = lax.broadcasted_iota(jnp.int32, (2 * CH, 256), 0)
-    p_col = lax.broadcasted_iota(jnp.int32, (2 * CH, 256), 1)
-    p_half = jnp.where(p_row >= CH, 1, 0)
-    p_out = p_row - CH * p_half
+    p_out = lax.broadcasted_iota(jnp.int32, (CH, 256), 0)
+    p_col = lax.broadcasted_iota(jnp.int32, (CH, 256), 1)
     p_owner = (p_out * 43691) >> 18
     p_slot = ((p_owner >> 1) ^ chip) + 8 * ((p_owner & 1) ^ core)
-    pick = jnp.where(p_slot * 16 + p_half * 8 + (p_out - 6 * p_owner) == p_col, 1.0, 0.0).astype(BF16)
+    p_row = p_out - 6 * p_owner
+    p_base = p_slot * 16 + p_row - p_col
+
+    def picker(shift, wanted=None):
+        hit = p_base + shift == 0
+        return jnp.where(hit if wanted is None else hit & wanted, 1.0, 0.0).astype(BF16)
+
+    pick_head = jnp.concatenate([picker(0), picker(6)], axis=0)
+    pick_tail = picker(12, p_row < 4)
+    pick_spare = jnp.concatenate([picker(8, p_row >= 4), picker(10, p_row >= 4)], axis=0)
 
     def assemble(k):
         for copy in f_copy[k]:
             copy.wait_recv()
-        packed = w_buf[k].reshape(256, HALF)
-        both = jnp.dot(pick, packed, preferred_element_type=F32).astype(BF16)
-        w_full[k, :, :HALF] = both[:CH]
-        w_full[k, :, HALF:] = both[CH:]
+        shards = w_buf[k].reshape(256, 8 * LT)
+        head = jnp.dot(pick_head, shards, preferred_element_type=F32).astype(BF16)
+        w_full[k, :, : 8 * LT] = head[:CH]
+        w_full[k, :, 8 * LT : 16 * LT] = head[CH:]
+        tail = jnp.dot(pick_tail, shards[:, : 5 * LT], preferred_element_type=F32)
+        spare = jnp.dot(pick_spare, shards[:, 5 * LT :], preferred_element_type=F32)
+        for n in range(5):
+            top, col = CH * (n % 2), n // 2
+            w_full[k, :, (16 + n) * LT : (17 + n) * LT] = (
+                tail[:, n * LT : (n + 1) * LT] + spare[top : top + CH, col * LT : (col + 1) * LT]
+            ).astype(BF16)
 
     def flip(k):
         for a in range(3):
@@ -324,7 +362,6 @@
         return left, cols[2, :, LT : 6 * LT]
 
     def start_term(m, pair):
-        term[m, :, 3 * KP :] = jnp.zeros((64, LT), F32)
         one_copy[m] = []
         for a in range(3):
             part = lax.dot_general(
@@ -343,21 +380,19 @@
             term[m, :, a * KP : (a + 1) * KP] += one_in[m, a].astype(F32)
         two_copy[m] = {}
         for j in FAR_FIRST:
-            two_out[m, j - 1] = jnp.concatenate(
-                [term[m, 8 * j : 8 * j + 8, :HALF], term[m, 8 * j : 8 * j + 8, HALF:]], axis=0
-            ).astype(BF16)
+            two_out[m, j - 1] = packed(term[m, 8 * j : 8 * j + 6, :]).astype(BF16)
             two_copy[m][j] = send(
                 two_out.at[m, j - 1], two_in.at[m, j - 1], two_send.at[m, j - 1],
                 two_recv.at[m, j - 1], chip_mate(j),
             )
 
     def sum_chips(m):
-        total = jnp.concatenate([term[m, :8, :HALF], term[m, :8, HALF:]], axis=0)
+        total = packed(term[m, :6, :])
         for j in reversed(FAR_FIRST):
             two_copy[m][j].wait_recv()
             total = total + two_in[m, j - 1].astype(F32)
-        tiles = [total[:8, n * LT : (n + 1) * LT] for n in range(11)]
-        return tiles + [total[8:, n * LT : (n + 1) * LT] for n in range(10)]
+        blank = jnp.zeros((2, LT), F32)
+        return [jnp.concatenate([tile, blank], axis=0) for tile in unpacked(total)]
 
     rows_far_first = (4, 5, 3, 2, 6, 7, 1)
     later = {}
@@ -442,19 +477,19 @@
     start_term(0, first_pair)
     reduce_chips(1)
     reduce_chips(0)
+
+    unroll_middle(3, g_one)
+    flip(0)
+    reduce_rows()
     unroll_edges(2)
-
-    unroll_middle(3, g_one)
     branch = convolve(w_full, 1, 2)
     outs = unpaired([occupied * (x_buf[0, j] + lanes_of(branch, j)) for j in range(4)], low)
     for j in range(4):
         bout_ref[0, 0, :, j * LT : (j + 1) * LT] = outs[j].astype(BF16)
     saves[0].start()
-    flip(0)
-    reduce_rows()
+    reduce_cols()
     unroll_edges(3)
     back = convolve(w_flip, 0, 3)
-    reduce_cols()
     outs = []
     for j in range(4):
         inner = act_vjp(n_buf[0, j], r_buf[0, j], occupied * lanes_of(back, j))
@@ -508,8 +543,8 @@
             pltpu.VMEM(features.shape, BF16),
             dma((6,)),
             dma((4,)),
-            pltpu.VMEM((2, 16, 16, HALF), BF16),
-            pltpu.VMEM((2, CH, 2 * HALF), BF16),
+            pltpu.VMEM((2, 16, 16, 8 * LT), BF16),
+            pltpu.VMEM((2, CH, 3 * KP), BF16),
             pltpu.VMEM((2, CH, 3 * KP), BF16),
             pltpu.VMEM((4, 2, CH, LT), BF16),
             pltpu.VMEM((4, 2, CH, LT), BF16),
@@ -519,11 +554,11 @@
             pltpu.VMEM((2, 4, 1, LT), F32),
             pltpu.VMEM((LT, 512), BF16),
             pltpu.VMEM((LT, 8 * LT), BF16),
-            pltpu.VMEM((2, 64, 2 * HALF), F32),
+            pltpu.VMEM((2, 64, 3 * KP), F32),
             pltpu.VMEM((2, 3, 64, KP), BF16),
             pltpu.VMEM((2, 3, 64, KP), BF16),
-            pltpu.VMEM((2, 7, 16, HALF), BF16),
-            pltpu.VMEM((2, 7, 16, HALF), BF16),
+            pltpu.VMEM((2, 7, 16, 8 * LT), BF16),
+            pltpu.VMEM((2, 7, 16, 8 * LT), BF16),
             pltpu.VMEM((8, 16, 3 * LT), F32),
             pltpu.VMEM((8, 16, 3 * LT), BF16),
             pltpu.VMEM((7, 16, 3 * LT), BF16),

time: 62.3 us -> 58.2 us (0.934)
  Pallas kernels: 60.8 us -> 56.8 us
    pallas_call x1, Pallas kernels: 59.1 us -> 55 us  [body(): pl.pallas_call(kernel, out_shape=(jax.ShapeDtypeStruct(features.shape, BF...]
where the time goes in v4:
time: 58.2 us; the launch traced here: 58.1 us
  Pallas kernels  56.8 us (98%)
  between operations  1.29 us (2%)
    pallas_call x1, Pallas kernels, body(): pl.pallas_call(kernel, out_shape=(jax.ShapeDtypeStruct(features.shape, BF...  55 us
    pallas_call x1, Pallas kernels, body(): pl.pallas_call(store, out_shape=tuple((jax.ShapeDtypeStruct(r.shape, r.dt...  1.79 us

profile of v4, /device:TPU:8, one launch (start us, length us, event | category | flops | bytes accessed | tf_op | source)
XLA Modules:
  0.0 58.1 jit_solution(151121560648420904)
XLA Ops:
  1.3 55.0 %shard_map.93 = (bf16[1,1,96,512]{3,2,1,0:T(8,128)(2,1)}, bf16[1,1,96,512]{3,2,1,0:T(8,128)(2,1)}, f32[6,2592]{1,0:T(8,128)}, f32[6,2592]{1,0:T(8,128)}) custom-call(bf16[1,1,96,512]{3,2,1,0:T(8,128)(2,1)} %feat_hbm.1, bf16[6,2592]{1,0:T(8,128)(2,1)} %wone_hbm.1, bf16[6,2592]{1,0:T(8,128)(2,1)} %wtwo_hbm.1, s32[1,1,6]{2,1,0:T(1,128)} %near_hbm.1, ...), custom_call_target="tpu_custom_call" | custom-call | tf_op jit(solution)/shard_map/pallas_call | solution.py:523
  56.3 1.8 %shard_map.94 = (bf16[1,1,96,512]{3,2,1,0:T(8,128)(2,1)}, bf16[1,1,96,512]{3,2,1,0:T(8,128)(2,1)}, f32[6,2592]{1,0:T(8,128)}, f32[6,2592]{1,0:T(8,128)}) custom-call(bf16[1,1,96,512]{3,2,1,0:T(8,128)(2,1)} %get-tuple-element.8.refs_0_, bf16[1,1,96,512]{3,2,1,0:T(8,128)(2,1)} %get-tuple-element.9.refs_1_, f32[6,2592]{1,0:T(8,128)} %get-tuple-element.10.refs_2_, ...), custom_call_target="tpu_custom_call" | custom-call | tf_op jit(solution)/shard_map/pallas_call | solution.py:576

commit v5 on v4

--- a/solution.py
+++ b/solution.py
@@ -391,8 +391,7 @@
         for j in reversed(FAR_FIRST):
             two_copy[m][j].wait_recv()
             total = total + two_in[m, j - 1].astype(F32)
-        blank = jnp.zeros((2, LT), F32)
-        return [jnp.concatenate([tile, blank], axis=0) for tile in unpacked(total)]
+        return total
 
     rows_far_first = (4, 5, 3, 2, 6, 7, 1)
     later = {}
@@ -400,14 +399,10 @@
     def reduce_rows():
         other = sum_chips(1)
         both = [sum_chips(0), other]
-        for p in range(7):
-            joined = jnp.concatenate(
-                [jnp.concatenate(tiles[3 * p : 3 * p + 3], axis=1) for tiles in both], axis=0
-            )
+        for p in range(8):
+            joined = jnp.concatenate([lanes_of(block, p) for block in both], axis=0)
             own_sum[p] = joined
             sum_src[p] = joined.astype(BF16)
-        own_sum[7] = jnp.zeros((16, 3 * LT), F32)
-        sum_src[7] = jnp.zeros((16, 3 * LT), BF16)
         later["y"] = [
             send(sum_src.at[xor(row, j)], sum_in.at[j - 1], y_send.at[j - 1], y_recv.at[j - 1], row_mate(j))
             for j in rows_far_first
@@ -438,9 +433,11 @@
     def finish():
         for copy in later["g"]:
             copy.wait_recv()
-        pieces = [whole[p].astype(F32) for p in range(7)]
         for m, out_ref in enumerate((gone_ref, gtwo_ref)):
-            flat = jnp.concatenate([one[8 * m : 8 * m + 6] for one in pieces], axis=1)
+            block = jnp.concatenate(
+                [whole[p, 16 * m : 16 * m + 16, :].astype(F32) for p in range(8)], axis=1
+            )
+            flat = jnp.concatenate(unpacked(block), axis=1)
             out_ref[...] = jnp.concatenate([flat[:, a * KP : a * KP + KA] for a in range(3)], axis=1)
 
     def silu_tiles(hidden):
@@ -473,9 +470,9 @@
         inner = act_vjp(n_buf[1, j], r_buf[1, j], occupied * lanes_of(back, j))
         g_one.append((occupied * inner).astype(BF16))
     send_halo(3, g_one[0], g_one[3])
+    reduce_chips(1)
     gp_buf[...] = spread_rows(g_one)
     start_term(0, first_pair)
-    reduce_chips(1)
     reduce_chips(0)
 
     unroll_middle(3, g_one)
@@ -559,12 +556,12 @@
             pltpu.VMEM((2, 3, 64, KP), BF16),
             pltpu.VMEM((2, 7, 16, 8 * LT), BF16),
             pltpu.VMEM((2, 7, 16, 8 * LT), BF16),
-            pltpu.VMEM((8, 16, 3 * LT), F32),
-            pltpu.VMEM((8, 16, 3 * LT), BF16),
-            pltpu.VMEM((7, 16, 3 * LT), BF16),
-            pltpu.VMEM((16, 3 * LT), BF16),
-            pltpu.VMEM((3, 16, 3 * LT), BF16),
-            pltpu.VMEM((8, 16, 3 * LT), WHOLE),
+            pltpu.VMEM((8, 32, LT), F32),
+            pltpu.VMEM((8, 32, LT), BF16),
+            pltpu.VMEM((7, 32, LT), BF16),
+            pltpu.VMEM((32, LT), BF16),
+            pltpu.VMEM((3, 32, LT), BF16),
+            pltpu.VMEM((8, 32, LT), WHOLE),
             dma((2, 7)), dma((2, 7)), dma((2, 8)), dma((2, 8)), dma((4, 2)), dma((4, 2)),
             dma((2, 3)), dma((2, 3)), dma((2, 7)), dma((2, 7)), dma((7,)), dma((7,)),
             dma((3,)), dma((3,)), dma((7,)), dma((7,)),

time: 58.2 us -> 56.9 us (0.978)
  Pallas kernels: 56.8 us -> 55.4 us
    pallas_call x1, Pallas kernels: 55 us -> 53.6 us  [body(): pl.pallas_call(kernel, out_shape=(jax.ShapeDtypeStruct(features.shape, BF...]
where the time goes in v5:
time: 56.9 us; the launch traced here: 56.7 us
  Pallas kernels  55.4 us (97%)
  between operations  1.29 us (2%)
    pallas_call x1, Pallas kernels, body(): pl.pallas_call(kernel, out_shape=(jax.ShapeDtypeStruct(features.shape, BF...  53.6 us
    pallas_call x1, Pallas kernels, body(): pl.pallas_call(store, out_shape=tuple((jax.ShapeDtypeStruct(r.shape, r.dt...  1.79 us

profile of v5, /device:TPU:8, one launch (start us, length us, event | category | flops | bytes accessed | tf_op | source)
XLA Modules:
  0.0 56.7 jit_solution(4015868324893939715)
XLA Ops:
  1.3 53.6 %shard_map.93 = (bf16[1,1,96,512]{3,2,1,0:T(8,128)(2,1)}, bf16[1,1,96,512]{3,2,1,0:T(8,128)(2,1)}, f32[6,2592]{1,0:T(8,128)}, f32[6,2592]{1,0:T(8,128)}) custom-call(bf16[1,1,96,512]{3,2,1,0:T(8,128)(2,1)} %feat_hbm.1, bf16[6,2592]{1,0:T(8,128)(2,1)} %wone_hbm.1, bf16[6,2592]{1,0:T(8,128)(2,1)} %wtwo_hbm.1, s32[1,1,6]{2,1,0:T(1,128)} %near_hbm.1, ...), custom_call_target="tpu_custom_call" | custom-call | tf_op jit(solution)/shard_map/pallas_call | solution.py:520
  54.9 1.8 %shard_map.94 = (bf16[1,1,96,512]{3,2,1,0:T(8,128)(2,1)}, bf16[1,1,96,512]{3,2,1,0:T(8,128)(2,1)}, f32[6,2592]{1,0:T(8,128)}, f32[6,2592]{1,0:T(8,128)}) custom-call(bf16[1,1,96,512]{3,2,1,0:T(8,128)(2,1)} %get-tuple-element.8.refs_0_, bf16[1,1,96,512]{3,2,1,0:T(8,128)(2,1)} %get-tuple-element.9.refs_1_, f32[6,2592]{1,0:T(8,128)} %get-tuple-element.10.refs_2_, ...), custom_call_target="tpu_custom_call" | custom-call | tf_op jit(solution)/shard_map/pallas_call | solution.py:573

commit v6 on v5

--- a/solution.py
+++ b/solution.py
@@ -160,7 +160,7 @@
         sent.append(copy)
         return copy
 
-    for k, ref in enumerate((wone_ref, wtwo_ref)):
+    def pack_weight(k, ref):
         loads[k].wait()
         rows = ref[...].astype(F32)
         gap = jnp.zeros((6, KP - KA), F32)
@@ -169,10 +169,13 @@
             parts += [rows[:, a * KA : (a + 1) * KA], gap]
         w_buf[k, 0] = packed(jnp.concatenate(parts, axis=1)).astype(BF16)
 
+    pack_weight(0, wone_ref)
     pl.semaphore_wait(barrier, len(mates))
 
     w_copy, f_copy = [], []
     for k in range(2):
+        if k == 1:
+            pack_weight(1, wtwo_ref)
         own = [send(w_buf.at[k, 0], w_buf.at[k, 8], f_send.at[k, 0], f_recv.at[k, 0], sibling)]
         f_copy.append(own)
         w_copy.append({

time: 56.9 us -> 56.9 us (level)
  no operation moved by 1% of the time
where the time goes in v6:
time: 56.9 us; the launch traced here: 56.7 us
  Pallas kernels  55.4 us (97%)
  between operations  1.29 us (2%)
    pallas_call x1, Pallas kernels, body(): pl.pallas_call(kernel, out_shape=(jax.ShapeDtypeStruct(features.shape, BF...  53.6 us
    pallas_call x1, Pallas kernels, body(): pl.pallas_call(store, out_shape=tuple((jax.ShapeDtypeStruct(r.shape, r.dt...  1.79 us

profile of v6, /device:TPU:8, one launch (start us, length us, event | category | flops | bytes accessed | tf_op | source)
XLA Modules:
  0.0 56.7 jit_solution(18043442446982615255)
XLA Ops:
  1.3 53.6 %shard_map.93 = (bf16[1,1,96,512]{3,2,1,0:T(8,128)(2,1)}, bf16[1,1,96,512]{3,2,1,0:T(8,128)(2,1)}, f32[6,2592]{1,0:T(8,128)}, f32[6,2592]{1,0:T(8,128)}) custom-call(bf16[1,1,96,512]{3,2,1,0:T(8,128)(2,1)} %feat_hbm.1, bf16[6,2592]{1,0:T(8,128)(2,1)} %wone_hbm.1, bf16[6,2592]{1,0:T(8,128)(2,1)} %wtwo_hbm.1, s32[1,1,6]{2,1,0:T(1,128)} %near_hbm.1, ...), custom_call_target="tpu_custom_call" | custom-call | tf_op jit(solution)/shard_map/pallas_call | solution.py:523
  54.9 1.8 %shard_map.94 = (bf16[1,1,96,512]{3,2,1,0:T(8,128)(2,1)}, bf16[1,1,96,512]{3,2,1,0:T(8,128)(2,1)}, f32[6,2592]{1,0:T(8,128)}, f32[6,2592]{1,0:T(8,128)}) custom-call(bf16[1,1,96,512]{3,2,1,0:T(8,128)(2,1)} %get-tuple-element.8.refs_0_, bf16[1,1,96,512]{3,2,1,0:T(8,128)(2,1)} %get-tuple-element.9.refs_1_, f32[6,2592]{1,0:T(8,128)} %get-tuple-element.10.refs_2_, ...), custom_call_target="tpu_custom_call" | custom-call | tf_op jit(solution)/shard_map/pallas_call | solution.py:576
